TPU v7x, 128 devices: a whole 4x4x4 slice. The times are simulated.
128 devices in a mesh: section: 16 (over z, y), tp: 8 (over x, core).
Axes of the slice: x: 4, y: 4, z: 4, core: 2. Of those that a mesh axis runs over, the one named last changes fastest.
Arguments:
- patch_states: bfloat16 [8192, 5120], P(('section', 'tp')), may hold values from -6 to 6
- merge_in: bfloat16 [5120, 5120], P(None, 'tp'), may hold values from -0.078125 to 0.078125
- merge_out: bfloat16 [5120, 8192], P('tp'), may hold values from -0.125 to 0.125
- kv_weight: bfloat16 [8192, 2048], P('tp'), may hold values from -0.09375 to 0.09375
- queries: bfloat16 [16, 16, 8192], P('section', None, 'tp'), may hold values from -90 to 90
- new_kv: bfloat16 [16, 16, 2048], P('section', None, 'tp'), may hold values from -8 to 8
- citations: int32 [128, 4], replicated, may hold values from 0 to 31, as said below
- lengths: int32 [128], replicated, may hold values from 3 to 4
- prefill_owner: int32 [128], replicated, may hold values from 0 to 15
- decode_owner: int32 [128], replicated, may hold values from 0 to 15, as said below
Outputs:
- attended: bfloat16 [16, 16, 8192], P('section', None, 'tp')
Inputs may be any that keep to these rules, and one draw needn't show every extreme that they name: `citations`: row w lists frames of one camera, newest first; frame f is encoded by section index f // 2; the first lengths[w] entries are read. Over the windows of one prefill owner, the frames read hold at most one frame of each section index and at most 8 frames in all; both bounds are met in every draw. `decode_owner`: no two windows with the same prefill owner have the same decode owner.
All inputs are finite; a program needn't handle non-finite values.
Results may differ from a plain program's by a relative error of at most 0.035.
Values may be sent and summed in bfloat16 or wider, within the bound.
A program may use at most 128 MiB of HBM per device.

v0:
```python
import math

import jax
import jax.numpy as jnp
from jax import lax
from jax.sharding import PartitionSpec as P

VIT = 1280
MERGED = 5120
KVH = 8
HD = 128
GRID = 16
FD = 2


def rotation_angles(offsets):
    half_width = HD // 2
    freq_slot = jnp.arange(half_width)
    inverse = jnp.exp(freq_slot.astype(jnp.float32) * (-2.0 * math.log(1000000.0) / HD))
    position = jnp.arange(GRID * GRID)
    height = (position // GRID).astype(jnp.float32)
    across = (position % GRID).astype(jnp.float32)
    first_cut = HD // 8
    second_cut = first_cut + 3 * HD // 16
    spatial = jnp.where(freq_slot[None, :] < second_cut, height[:, None], across[:, None])
    temporal = offsets.astype(jnp.float32)[..., None, None]
    placed = jnp.where(freq_slot < first_cut, temporal, spatial)
    return placed * inverse


def rotate_keys(key_rows, angles):
    half_width = key_rows.shape[-1] // 2
    cosine = jnp.cos(angles)
    sine_part = jnp.sin(angles)
    first_half = key_rows[..., :half_width]
    second_half = key_rows[..., half_width:]
    return jnp.concatenate(
        [
            first_half * cosine - second_half * sine_part,
            second_half * cosine + first_half * sine_part,
        ],
        axis=-1,
    )


def head_terms(inputs, kv_weight, head_count):
    width = kv_weight.shape[1] // KVH
    product = jnp.dot(inputs, kv_weight, preferred_element_type=jnp.float32)
    return product.reshape(inputs.shape[0], head_count, width).transpose(1, 0, 2)


def attend_pages(query_block, pair_block, pages, counts, present, heads_local):
    sections = query_block.shape[0]
    heads_per = query_block.shape[1] // (heads_local * HD)
    list_pos = jnp.arange(pages.shape[1])
    query_rows = query_block.reshape(sections, heads_local, heads_per, HD)
    own_pair = pair_block.reshape(sections, heads_local, 2, HD)
    inv_root = 1.0 / math.sqrt(HD)
    scores = (
        jnp.einsum(
            "ohgd,ojhtd->ohgjt", query_rows, pages[..., 0, :], preferred_element_type=jnp.float32
        )
        * inv_root
    )
    usable = (list_pos[None, :] < counts[:, None])[:, None, None, :, None]
    scores = jnp.where(usable, scores, -jnp.inf)
    own_score = (
        jnp.einsum(
            "ohgd,ohd->ohg", query_rows, own_pair[:, :, 0, :], preferred_element_type=jnp.float32
        )
        * inv_root
    )
    highest = jnp.maximum(jnp.max(scores, axis=(3, 4)), own_score)
    weights = jnp.exp(scores - highest[..., None, None])
    own_weight = jnp.exp(own_score - highest)
    denominator = jnp.sum(weights, axis=(3, 4)) + own_weight
    weights = (weights / denominator[..., None, None]).astype(jnp.bfloat16)
    own_weight = (own_weight / denominator).astype(jnp.bfloat16)
    result = jnp.einsum(
        "ohgjt,ojhtd->ohgd", weights, pages[..., 1, :], preferred_element_type=jnp.float32
    )
    result = (
        result
        + own_weight.astype(jnp.float32)[..., None]
        * own_pair[:, :, 1, :].astype(jnp.float32)[:, :, None, :]
    )
    result = jnp.where(present[:, None, None, None], result, 0.0)
    return result.reshape(sections, -1).astype(jnp.bfloat16)


def shards(
    patch_states,
    merge_in,
    merge_out,
    kv_weight,
    queries,
    new_kv,
    citations,
    lengths,
    prefill_owner,
    decode_owner,
):
    sections = lax.axis_size("section")
    heads_local = KVH // lax.axis_size("tp")
    myself = lax.axis_index("section")
    frame_tokens = GRID * GRID
    row_count = patch_states.shape[0]
    blocks = patch_states.astype(jnp.float32).reshape(row_count, -1, VIT)
    centered = blocks - jnp.mean(blocks, axis=-1, keepdims=True)
    variance = jnp.mean(centered * centered, axis=-1, keepdims=True)
    normed = (
        (centered * lax.rsqrt(variance + 1e-06)).reshape(row_count, MERGED).astype(jnp.bfloat16)
    )
    hidden = jax.nn.gelu(
        jnp.dot(
            lax.all_gather(normed, "tp", axis=0, tiled=True),
            merge_in,
            preferred_element_type=jnp.float32,
        ),
        approximate=False,
    ).astype(jnp.bfloat16)
    partial_rows = jnp.dot(hidden, merge_out, preferred_element_type=jnp.float32)
    merged = lax.psum_scatter(partial_rows, "tp", scatter_dimension=1, tiled=True).astype(
        jnp.bfloat16
    )
    feature_width = merged.shape[1]
    local_frames = merged.reshape(FD, frame_tokens, feature_width)
    cite_count = citations.shape[1]
    window_total = citations.shape[0]
    window_ids = jnp.arange(window_total)
    section_ids = jnp.arange(sections)
    list_pos = jnp.arange(cite_count)
    is_read = list_pos[None, :] < lengths[:, None]
    source_section = citations // FD
    frame_within = citations % FD
    mine_read = is_read & (source_section == myself)
    outgoing_hits = mine_read[:, :, None] & (
        prefill_owner[:, None, None] == section_ids[None, None, :]
    )
    wanted = jnp.any(outgoing_hits, axis=(0, 1))
    wanted_frame = jnp.max(jnp.where(outgoing_hits, frame_within[:, :, None], 0), axis=(0, 1))
    owned_read = is_read & (prefill_owner[:, None] == myself)
    feeding = jnp.any(
        owned_read[:, :, None] & (source_section[:, :, None] == section_ids[None, None, :]),
        axis=(0, 1),
    )
    outgoing = jnp.where(
        wanted[:, None, None], local_frames[wanted_frame], jnp.zeros((), jnp.bfloat16)
    )
    arrived = lax.all_to_all(outgoing, "section", split_axis=0, concat_axis=0, tiled=True)
    capacity = 2 * cite_count
    compact_slot = jnp.cumsum(feeding.astype(jnp.int32)) - 1
    matches = (compact_slot[None, :] == jnp.arange(capacity)[:, None]) & feeding[None, :]
    picked = jnp.sum(jnp.where(matches, section_ids[None, :], 0), axis=1)
    gathered_rows = arrived[picked].reshape(capacity * frame_tokens, feature_width)
    projected = lax.psum_scatter(
        head_terms(gathered_rows, kv_weight, heads_local * lax.axis_size("tp")),
        "tp",
        scatter_dimension=0,
        tiled=True,
    )
    page_table = (
        projected.astype(jnp.bfloat16)
        .reshape(heads_local, capacity, frame_tokens, -1)
        .transpose(1, 0, 2, 3)
    )
    sending = (prefill_owner[None, :] == myself) & (decode_owner[None, :] == section_ids[:, None])
    present = jnp.any(sending, axis=1)
    chosen = jnp.sum(jnp.where(sending, window_ids[None, :], 0), axis=1)
    chosen_cited = citations[chosen]
    chosen_count = jnp.where(present, lengths[chosen], 0)
    live_page = list_pos[None, :] < chosen_count[:, None]
    page_slots = compact_slot[chosen_cited // FD]
    fetched = page_table[page_slots.reshape(-1)].reshape(
        sections, cite_count, heads_local, frame_tokens, 2, HD
    )
    angles = rotation_angles(chosen_count[:, None] - 1 - list_pos[None, :])
    page_keys = rotate_keys(
        fetched[..., 0, :].astype(jnp.float32), angles[:, :, None, :, :]
    ).astype(jnp.bfloat16)
    stacked = jnp.stack([page_keys, fetched[..., 1, :]], axis=4)
    stacked = jnp.where(
        live_page[:, :, None, None, None, None], stacked, jnp.zeros((), jnp.bfloat16)
    )
    query_rows = queries[0]
    pair_rows = new_kv[0]
    received = lax.all_to_all(stacked, "section", split_axis=0, concat_axis=0, tiled=True)
    incoming = (decode_owner[None, :] == myself) & (prefill_owner[None, :] == section_ids[:, None])
    served = jnp.any(incoming, axis=1)
    arriving = jnp.sum(jnp.where(incoming, window_ids[None, :], 0), axis=1)
    served_count = jnp.where(served, lengths[arriving], 0)
    return attend_pages(query_rows, pair_rows, received, served_count, served, heads_local)[None]


def solution(mesh):
    return jax.shard_map(
        shards,
        mesh=mesh,
        in_specs=(
            P(("section", "tp"), None),
            P(None, "tp"),
            P("tp", None),
            P("tp", None),
            P("section", None, "tp"),
            P("section", None, "tp"),
            P(),
            P(),
            P(),
            P(),
        ),
        out_specs=P("section", None, "tp"),
        check_vma=False,
    )
```

profile of v0, /device:TPU:1, one launch (start us, length us, event | category | flops | bytes accessed | tf_op | source)
XLA Modules:
  0.0 622.2 jit_solution(3375030237121102828)
XLA Ops:
  6.5 1.9 reshape.581
  8.4 0.2 reduce_sum.64
  8.7 0.5 multiply_reduce_fusion
  9.2 0.2 mul.104
  9.4 0.2 copy.77
  9.6 0.2 sub.71
  9.9 0.2 copy.76
  10.1 0.8 copy-done.1
  11.0 1.0 multiply_convert_fusion
  12.0 0.0 reduce-scatter.3.cloned.1.call-start
  12.0 40.2 %all-gather.2.cloned.1.call-done = bf16[512,5120]{1,0:T(8,128)(2,1)} async-done(((bf16[64,5120]{1,0:T(8,128)(2,1)}), bf16[512,5120]{1,0:T(8,128)(2,1)}) %all-gather.2.cloned.1.call-update) | async-done | bytes 5242896 | tf_op jit(solution)/shard_map/all_gather | solution.py:116
  52.2 23.5 %fusion.24 = f32[512,8192]{1,0:T(8,128)} fusion(bf16[640,8192]{1,0:T(8,128)(2,1)} %param.12, bf16[512,5120]{1,0:T(8,128)(2,1)} %all-gather.2.cloned.1.call-done, bf16[5120,640]{1,0:T(8,128)(2,1)} %param.11), kind=kOutput, calls=%fused_computation.52 | convolution fusion | flops 8745451520 | bytes 39059456 | tf_op jit(solution)/shard_map/dot_general | solution.py:122
  75.7 0.0 reduce-scatter.3.cloned.1.call-update
  75.7 0.6 copy-done.5
  76.4 0.0 copy-done.3
  76.4 0.1 fusion.59
  76.6 0.1 and_reduce_fusion
  76.7 90.0 %reduce-scatter.3.cloned.1.call-done = f32[512,1024]{1,0:T(8,128)} async-done(((f32[512,8192]{1,0:T(8,128)}), f32[512,1024]{1,0:T(8,128)}) %reduce-scatter.3.cloned.1.call-update) | async-done | bytes 2097168 | tf_op jit(solution)/shard_map/reduce_scatter | solution.py:123
  166.7 1.7 convert_element_type.119
  168.4 4.6 gather_fusion.2
  173.1 7.2 %broadcast_select_fusion = bf16[16,256,1024]{2,1,0:T(8,128)(2,1)} fusion(bf16[16,256,1024]{2,1,0:T(8,128)(2,1)} %gather_fusion.2, pred[16]{0:T(512)(128)(4,1)S(1)} %and_reduce_fusion), kind=kLoop, calls=%fused_computation.8 | loop fusion | flops 4194304 | bytes 16777232 | tf_op jit(solution)/shard_map/jit(_where)/select_n | solution.py:147
  180.3 6.6 %all-to-all-start = ((bf16[16,256,1024]{2,1,0:T(8,128)(2,1)}), bf16[16,256,1024]{2,1,0:T(8,128)(2,1)}, u32[]{:S(2)}, u32[]{:S(2)}) async-start(bf16[16,256,1024]{2,1,0:T(8,128)(2,1)} %broadcast_select_fusion), calls=%async_computation.1 | async-start | bytes 16777216 | tf_op jit(solution)/shard_map/all_to_all | solution.py:150
  186.9 0.2 reduce-scatter.5.cloned.1.call-start
  187.2 0.1 fusion.62
  187.3 0.1 copy.58
  187.4 6.4 %copy.72 = bf16[2048,1024]{1,0:T(8,128)(2,1)} copy(bf16[2048,1024]{0,1:T(8,128)(2,1)} %bitcast.136) | data formatting | bytes 8388608 | tf_op jit(solution)/shard_map/dot_general | solution.py:48
  193.8 0.1 add_reduce_fusion
  193.9 0.1 select_reduce_fusion.2
  194.1 114.5 %all-to-all-done = bf16[16,256,1024]{2,1,0:T(8,128)(2,1)} async-done(((bf16[16,256,1024]{2,1,0:T(8,128)(2,1)}), bf16[16,256,1024]{2,1,0:T(8,128)(2,1)}, u32[]{:S(2)}, u32[]{:S(2)}) %all-to-all-start) | async-done | bytes 8388640 | tf_op jit(solution)/shard_map/all_to_all | solution.py:150
  308.5 6.2 gather_fusion.3
  314.7 15.2 %convolution_bitcast_fusion = f32[8,2048,256]{2,1,0:T(8,128)} fusion(bf16[2048,1024,1]{1,0,2:T(8,128)(2,1)} %bitcast.138, bf16[8,256,1024]{2,1,0:T(8,128)(2,1)} %bitcast.137), kind=kOutput, calls=%fused_computation.9 | convolution fusion | flops 8589934592 | bytes 25165824 | tf_op jit(solution)/shard_map/dot_general | solution.py:48
  329.9 0.1 copy.60
  330.0 0.5 copy-done.6
  330.5 0.1 select_reduce_fusion
  330.7 0.7 gather_fusion.1
  331.3 0.6 gather_fusion.4
  331.9 0.1 copy.61
  332.0 0.1 copy.62
  332.1 0.1 reshape.635
  332.2 0.8 gather_fusion.5
  333.0 0.1 fusion.67
  333.2 0.1 iota_compare_fusion.3
  333.2 0.1 subtract_convert_fusion.1
  333.3 0.1 broadcast_select_fusion.1
  333.4 90.4 %reduce-scatter.5.cloned.1.call-done = f32[1,2048,256]{2,1,0:T(8,128)} async-done(((f32[8,2048,256]{2,1,0:T(8,128)}), f32[1,2048,256]{2,1,0:T(8,128)}) %reduce-scatter.5.cloned.1.call-update) | async-done | bytes 2097168 | tf_op jit(solution)/shard_map/reduce_scatter | solution.py:156
  423.7 1.7 convert_element_type.122
  425.4 5.4 gather_fusion.6
  430.9 11.9 %copy.63 = bf16[64,256,256]{1,2,0:T(8,128)(2,1)} copy(bf16[64,256,256]{2,1,0:T(8,128)(2,1)} %gather_fusion.6) | data formatting | bytes 16777216 | tf_op jit(solution)/shard_map/gather | solution.py:174
  442.7 4.1 fusion.2
  446.8 16.1 %fusion.5 = (bf16[16,4,256,1,64]{2,4,1,0,3:T(8,128)(2,1)S(1)}, bf16[16,4,256,1,64]{2,4,1,0,3:T(8,128)(2,1)S(1)}) fusion(f32[16,4,1,256,128]{3,4,1,0,2:T(8,128)S(1)} %get-tuple-element.11, f32[64]{0:T(128)S(1)} %multiply_exponential_fusion, f32[256,64]{0,1:T(8,128)S(1)} %broadcast_select_fusion.1, f32[16,4]{1,0:T(8,128)S(1)} %subtract_convert_fusion.1, ...), kind=kLoop, calls=%fused_computation.22 | loop fusion | flops 10485760 | bytes 12649024 | tf_op jit(solution)/shard_map/concatenate | solution.py:37
  462.9 0.5 maximum_bitcast_fusion
  463.4 4.2 maximum_select_fusion
  467.6 12.3 %copy.65 = bf16[16,4,1,256,2,128]{5,3,1,4,2,0:T(8,128)(2,1)} copy(bf16[16,4,1,256,2,128]{3,5,4,1,0,2:T(8,128)(2,1)} %maximum_select_fusion) | data formatting | bytes 16777216 | tf_op jit(solution)/shard_map/jit(_where)/select_n | solution.py:182
  479.9 6.8 %all-to-all-start.1 = ((bf16[16,4,1,256,2,128]{5,3,1,4,2,0:T(8,128)(2,1)}), bf16[16,4,1,256,2,128]{5,3,1,4,2,0:T(8,128)(2,1)}, u32[]{:S(2)}, u32[]{:S(2)}) async-start(bf16[16,4,1,256,2,128]{5,3,1,4,2,0:T(8,128)(2,1)} %copy.65), calls=%async_computation.3 | async-start | bytes 16777216 | tf_op jit(solution)/shard_map/all_to_all | solution.py:187
  486.7 0.1 select_reduce_fusion.1
  486.9 0.7 gather_fusion
  487.6 0.1 fusion.65
  487.7 0.1 iota_compare_fusion.4
  487.8 0.1 fusion.63
  487.9 120.4 %all-to-all-done.1 = bf16[16,4,1,256,2,128]{5,3,1,4,2,0:T(8,128)(2,1)} async-done(((bf16[16,4,1,256,2,128]{5,3,1,4,2,0:T(8,128)(2,1)}), bf16[16,4,1,256,2,128]{5,3,1,4,2,0:T(8,128)(2,1)}, u32[]{:S(2)}, u32[]{:S(2)}) %all-to-all-start.1) | async-done | bytes 8388640 | tf_op jit(solution)/shard_map/all_to_all | solution.py:187
  608.4 3.5 fusion.116
  611.8 0.2 fusion.56
  612.1 2.9 fusion.23
  615.0 0.6 convert_element_type.133
  (45 shorter events, 0.3 us)
Async XLA Ops:
  6.5 45.7 %all-gather.2.cloned.1.call-start = ((), (), s32[]{:S(2)}) async-start(), calls=%async_computation.4 | async-start | bytes 5898240 | tf_op jit(solution)/shard_map/all_gather | solution.py:116
  9.9 1.1 copy-start.1
  12.0 154.7 %reduce-scatter.3.cloned.1.call-start = ((), (), s32[]{:S(2)}) async-start(), calls=%async_computation.5 | async-start | bytes 18874368 | tf_op jit(solution)/shard_map/reduce_scatter | solution.py:123
  75.7 0.7 copy-start.5
  75.7 0.7 copy-start.3
  75.7 0.7 copy-start
  180.3 128.2 %all-to-all-start = ((bf16[16,256,1024]{2,1,0:T(8,128)(2,1)}), bf16[16,256,1024]{2,1,0:T(8,128)(2,1)}, u32[]{:S(2)}, u32[]{:S(2)}) async-start(bf16[16,256,1024]{2,1,0:T(8,128)(2,1)} %broadcast_select_fusion), calls=%async_computation.1 | async-start | bytes 16777216 | tf_op jit(solution)/shard_map/all_to_all | solution.py:150
  186.9 236.8 %reduce-scatter.5.cloned.1.call-start = ((), (), s32[]{:S(2)}) async-start(), calls=%async_computation.6 | async-start | bytes 18874368 | tf_op jit(solution)/shard_map/reduce_scatter | solution.py:156
  329.9 0.7 copy-start.6
  479.9 7.7 %copy-start.2 = (bf16[1,16,1024]{2,1,0:T(8,128)(2,1)S(1)}, bf16[1,16,1024]{2,1,0:T(8,128)(2,1)}, u32[]{:S(2)}) copy-start(bf16[1,16,1024]{2,1,0:T(8,128)(2,1)} %param.14) | copy-start | bytes 98308
  479.9 7.7 %copy-start.4 = (bf16[1,16,256]{2,1,0:T(8,128)(2,1)S(1)}, bf16[1,16,256]{2,1,0:T(8,128)(2,1)}, u32[]{:S(2)}) copy-start(bf16[1,16,256]{2,1,0:T(8,128)(2,1)} %param.15) | copy-start | bytes 24580
  479.9 128.5 %all-to-all-start.1 = ((bf16[16,4,1,256,2,128]{5,3,1,4,2,0:T(8,128)(2,1)}), bf16[16,4,1,256,2,128]{5,3,1,4,2,0:T(8,128)(2,1)}, u32[]{:S(2)}, u32[]{:S(2)}) async-start(bf16[16,4,1,256,2,128]{5,3,1,4,2,0:T(8,128)(2,1)} %copy.65), calls=%async_computation.3 | async-start | bytes 16777216 | tf_op jit(solution)/shard_map/all_to_all | solution.py:187
Sparse Core Ops, SparseCore 0:
  12.1 40.0 all-gather.1
  75.9 90.7 reduce-scatter.2
  330.0 93.6 reduce-scatter.4
where the time goes:
time: 630 us; the launch traced here: 622 us
  waiting for transfers between devices  456 us (72%)
  local copies, waits for them, and re-layouts  55.4 us (9%)
  matrix products  45.1 us (7%)
  other arithmetic  39.1 us (6%)
  starting transfers between devices  13.7 us (2%)
  between operations  13.4 us (2%)
    all_to_all x1, waiting for transfers between devices, shards(): lax.all_to_all(stacked, 'section', split_axis=0, concat_axis=0, tiled=True)  120 us
    all_to_all x1, waiting for transfers between devices, shards(): lax.all_to_all(outgoing, 'section', split_axis=0, concat_axis=0, tiled=True)  114 us
    reduce_scatter x1, waiting for transfers between devices, shards(): lax.psum_scatter(head_terms(gathered_rows, kv_weight, heads_local * lax.a...  90.4 us
    reduce_scatter x1, waiting for transfers between devices, shards(): lax.psum_scatter(partial_rows, 'tp', scatter_dimension=1, tiled=True)  90 us
    all_gather x1, waiting for transfers between devices, shards(): lax.all_gather(normed, 'tp', axis=0, tiled=True)  40.2 us
    dot_general x1, matrix products, shards(): jnp.dot(hidden, merge_out, preferred_element_type=jnp.float32)  23.5 us
    gather x2, local copies, waits for them, and re-layouts, shards(): page_table[page_slots.reshape(-1)]  17.3 us
    concatenate x1, other arithmetic, rotate_keys(): jnp.concatenate([first_half * cosine - second_half * sine_part, second_ha...  16.1 us
  transfers between devices with their start and end apart: 5, of which 5 were waited for; matrix products, arithmetic and copies ran while one was open for 2% of the time, Pallas kernels for 0%

commit v1 on v0

v1 whole, which is shorter than its diff:
```python
import math

import jax
import jax.numpy as jnp
import numpy as np
from jax import lax
from jax.experimental import pallas as pl
from jax.experimental.pallas import tpu as pltpu
from jax.sharding import PartitionSpec as P

F32 = jnp.float32
BF16 = jnp.bfloat16
VIT = 1280
HD = 128
GRID = 16
NS = 16
CITE = 4
ROWS = 64
GROUP = 128
TOKENS = 512
KIN = 5120
HU = 640
KVB = 1024
HALF = HU // 2
QUARTER = HU // 4
PART = 144


def tables():
    slot = np.arange(HD // 2)
    inverse = np.exp(slot.astype(np.float32) * np.float32(-2.0 * math.log(1000000.0) / HD)).astype(np.float32)
    token = np.arange(GRID * GRID)
    height = (token // GRID).astype(np.float32)
    across = (token % GRID).astype(np.float32)
    first = HD // 8
    second = first + 3 * HD // 16
    spatial = np.where(slot[None, :] < second, height[:, None], across[:, None])
    spatial = np.where(slot[None, :] < first, np.float32(0.0), spatial) * inverse[None, :]
    cosine, sine = np.cos(spatial), np.sin(spatial)
    keys = np.stack([np.concatenate([cosine, cosine], 1), np.concatenate([-sine, sine], 1)])
    steps = np.arange(CITE).astype(np.float32)[:, None] * inverse[None, :]
    steps = np.where(slot[None, :] < first, steps, np.float32(0.0))
    cosine, sine = np.cos(steps), np.sin(steps)
    asks = np.stack([np.concatenate([cosine, cosine], 1), np.concatenate([sine, -sine], 1)])
    return keys.astype(np.float32), asks.astype(np.float32)


class Counter:
    def __init__(self):
        self.n = 0

    def take(self, k=1):
        first = self.n
        self.n += k
        return first


N_SEND = 160
N_RECV = 160
N_LOCAL = 8


def kernel(
    patch, w1, w2, kvw, q, nkv, meta, ktab, qtab, out,
    rows, w1v, w2v, kvg, wacc, wg, hacc, mine, psend, precv, h1s, h1r, h2s, h2r,
    kbuf, vbuf, vt, qg, osend, orecv, ssem, rsem, lsem,
):
    s = lax.axis_index("section")
    t = lax.axis_index("tp")
    x, c = t // 2, t % 2
    z, y = s // 4, s % 4
    mate = 2 * x + (1 - c)
    cr, cl, co = (x + 1) % 4, (x + 3) % 4, (x + 2) % 4
    xr, xl, xo = 2 * cr + c, 2 * cl + c, 2 * co + c
    yn, yp, yo = (y + 1) % 4, (y + 3) % 4, (y + 2) % 4
    zn, zp, zo = (z + 1) % 4, (z + 3) % 4, (z + 2) % 4
    sends, recvs = Counter(), Counter()
    pending = []

    def to_tp(who):
        return {"tp": who}

    def to_section(who):
        return {"section": who}

    def start(src, dst, slot, dev):
        copy = pltpu.make_async_remote_copy(
            src_ref=src, dst_ref=dst, send_sem=ssem.at[sends.take()], recv_sem=rsem.at[slot],
            device_id=dev, device_id_type=pl.DeviceIdType.MESH,
        )
        copy.start()
        pending.append(copy)

    def arrive(dst, slot):
        pltpu.make_async_remote_copy(
            src_ref=dst, dst_ref=dst, send_sem=ssem.at[0], recv_sem=rsem.at[slot],
            device_id=to_tp(mate), device_id_type=pl.DeviceIdType.MESH,
        ).wait_recv()

    load1 = pltpu.make_async_copy(w1, w1v, lsem.at[0])
    load2 = pltpu.make_async_copy(w2, w2v, lsem.at[1])
    cols = pl.ds(pl.multiple_of(s * HD, HD), HD)

    def kv_at(b, h=None):
        if h is None:
            return kvg.at[pl.ds(pl.multiple_of(b * KVB, KVB), KVB), :]
        return kvg.at[pl.ds(pl.multiple_of(b * KVB + h * (KVB // 2), KVB // 2), KVB // 2), :]

    def kv_own(h=None):
        if h is None:
            return kvw.at[:, cols]
        return kvw.at[pl.ds(h * (KVB // 2), KVB // 2), cols]

    def rows_at(b, h=None):
        if h is None:
            return rows.at[pl.ds(pl.multiple_of(b * ROWS, ROWS), ROWS), :]
        return rows.at[pl.ds(pl.multiple_of(b * ROWS + h * (ROWS // 2), ROWS // 2), ROWS // 2), :]

    load3 = pltpu.make_async_copy(kv_own(), kv_at(t), lsem.at[2])
    load4 = pltpu.make_async_copy(q, qg.at[s], lsem.at[3])
    load3.start()
    load4.start()
    load2.start()
    load1.start()

    barrier = pltpu.get_barrier_semaphore()
    for who in (mate, xr, xl):
        pl.semaphore_signal(barrier, inc=1, device_id=to_tp(who), device_id_type=pl.DeviceIdType.MESH)

    @pl.loop(1, NS)
    def _(i):
        pl.semaphore_signal(
            barrier, inc=1, device_id=to_section((s + i) % NS), device_id_type=pl.DeviceIdType.MESH
        )

    pl.semaphore_wait(barrier, 3 + NS - 1)

    class Ring:
        def __init__(self, at):
            self.at = at
            self.base = recvs.take(10)

        def open(self, own):
            b = self.base
            start(own(0), self.at(t, 0), b + 0, to_tp(xr))
            start(own(1), self.at(t, 1), b + 3, to_tp(xl))
            start(own(1), self.at(t, 1), b + 1, to_tp(xr))
            start(own(0), self.at(t, 0), b + 2, to_tp(xl))
            start(own(None), self.at(t), b + 6, to_tp(mate))

        def forward(self):
            b = self.base
            arrive(self.at(xl, 0), b + 0)
            start(self.at(xl, 0), self.at(xl, 0), b + 4, to_tp(xr))
            arrive(self.at(xr, 1), b + 3)
            start(self.at(xr, 1), self.at(xr, 1), b + 5, to_tp(xl))

        def near(self):
            b = self.base
            arrive(self.at(xl, 1), b + 1)
            start(self.at(xl), self.at(xl), b + 7, to_tp(mate))
            arrive(self.at(xr, 0), b + 2)
            start(self.at(xr), self.at(xr), b + 8, to_tp(mate))

        def far(self):
            b = self.base
            arrive(self.at(xo, 0), b + 4)
            arrive(self.at(xo, 1), b + 5)
            start(self.at(xo), self.at(xo), b + 9, to_tp(mate))

        def mates(self, k):
            chip = (x, cl, cr, co)[k]
            arrive(self.at(2 * chip + (1 - c)), self.base + 6 + k)

    kv_ring = Ring(kv_at)
    kv_ring.open(kv_own)

    q_base = recvs.take(NS)
    q_send = sends.take(NS)

    def q_copy(i):
        return pltpu.make_async_remote_copy(
            src_ref=q, dst_ref=qg.at[s], send_sem=ssem.at[q_send + i], recv_sem=rsem.at[q_base + i],
            device_id=to_section((s + i) % NS), device_id_type=pl.DeviceIdType.MESH,
        )

    @pl.loop(1, NS)
    def _(i):
        q_copy(i).start()

    for b in range(KIN // VIT):
        span = pl.ds(b * VIT, VIT)
        block = patch[:, span].astype(F32)
        centered = block - jnp.mean(block, axis=-1, keepdims=True)
        variance = jnp.mean(centered * centered, axis=-1, keepdims=True)
        rows[pl.ds(pl.multiple_of(t * ROWS, ROWS), ROWS), span] = (
            centered * lax.rsqrt(variance + 1e-06)
        ).astype(BF16)

    kv_ring.forward()
    row_ring = Ring(rows_at)
    row_ring.open(lambda h: rows_at(t, h))

    def w_step(b, first=False):
        part = jnp.dot(
            w2v[:, pl.ds(pl.multiple_of(b * KVB, KVB), KVB)],
            kvg[pl.ds(pl.multiple_of(b * KVB, KVB), KVB), :],
            preferred_element_type=F32,
        )
        if first:
            wacc[...] = part
        else:
            wacc[...] += part

    load3.wait()
    load2.wait()
    w_step(t, first=True)
    kv_ring.mates(0)
    w_step(mate)
    kv_ring.near()
    w_step(xl)
    w_step(xr)
    kv_ring.far()
    w_step(xo)
    kv_ring.mates(1)
    w_step(2 * cl + (1 - c))
    kv_ring.mates(2)
    w_step(2 * cr + (1 - c))
    kv_ring.mates(3)
    w_step(2 * co + (1 - c))

    def lanes(yy):
        return pl.ds(pl.multiple_of((yy % 2) * HD, HD), HD)

    def block_at(zz, yy, r0, n):
        return wg.at[zz, yy // 2, pl.ds(r0, n), lanes(yy)]

    def line_at(zz, r0, n):
        return wg.at[zz, :, pl.ds(r0, n), :]

    def column_at(yy, r0, n):
        return wg.at[:, yy // 2, pl.ds(r0, n), lanes(yy)]

    def sec(zz, yy):
        return to_section(zz * 4 + yy)

    wg[z, y // 2, :, lanes(y)] = wacc[...].astype(BF16)

    class Cross:
        def __init__(self, at, me, nxt, prv, opp, dev_n, dev_p, r0):
            self.at, self.me, self.nxt, self.prv, self.opp = at, me, nxt, prv, opp
            self.dev_n, self.dev_p, self.r0 = dev_n, dev_p, r0
            self.base = recvs.take(4)

        def open(self):
            b, own = self.base, self.at(self.me, self.r0, HALF)
            start(own, own, b + 0, self.dev_n)
            start(own, own, b + 1, self.dev_p)

        def forward(self):
            b = self.base
            arrive(self.at(self.prv, self.r0, HALF), b + 0)
            low = self.at(self.prv, self.r0, QUARTER)
            start(low, low, b + 2, self.dev_n)
            arrive(self.at(self.nxt, self.r0, HALF), b + 1)
            high = self.at(self.nxt, self.r0 + QUARTER, QUARTER)
            start(high, high, b + 3, self.dev_p)

        def finish(self):
            b = self.base
            arrive(self.at(self.opp, self.r0, QUARTER), b + 2)
            arrive(self.at(self.opp, self.r0 + QUARTER, QUARTER), b + 3)

    y_first = Cross(lambda yy, r, n: block_at(z, yy, r, n), y, yn, yp, yo, sec(z, yn), sec(z, yp), 0)
    z_first = Cross(lambda zz, r, n: block_at(zz, y, r, n), z, zn, zp, zo, sec(zn, y), sec(zp, y), HALF)
    z_then = Cross(line_at, z, zn, zp, zo, sec(zn, y), sec(zp, y), 0)
    y_then = Cross(column_at, y, yn, yp, yo, sec(z, yn), sec(z, yp), HALF)
    y_first.open()
    z_first.open()

    def hidden(g):
        r = pl.ds(pl.multiple_of(g * GROUP, GROUP), GROUP)

        def part(k):
            span = pl.ds(pl.multiple_of(k * 1024, 1024), 1024)
            return jnp.dot(rows[r, span], w1v[span, :], preferred_element_type=F32)

        hacc[g] = part(0)

        @pl.loop(1, KIN // 1024)
        def _(k):
            hacc[g] += part(k)

    p_base = recvs.take(4)
    p_send = sends.take(4)

    def pair_copy(k, g):
        return pltpu.make_async_remote_copy(
            src_ref=psend.at[g], dst_ref=precv.at[g], send_sem=ssem.at[p_send + k],
            recv_sem=rsem.at[p_base + k], device_id=to_tp(mate), device_id_type=pl.DeviceIdType.MESH,
        )

    def project(k, g):
        pre = hacc[g]
        hid = (0.5 * pre * (1.0 + lax.erf(pre * np.float32(math.sqrt(0.5))))).astype(BF16)
        for xx in range(4):
            psend[g, xx] = jnp.dot(hid, wg[xx, 1 - c], preferred_element_type=F32).astype(BF16)
        pair_copy(k, g).start()
        for xx in range(4):
            mine[g, xx] = jnp.dot(hid, wg[xx, c], preferred_element_type=F32)

    h1_base = recvs.take(8)
    h1_send = sends.take(8)
    h2_base = recvs.take(8)
    h2_send = sends.take(8)

    def hop(src, dst, ssl, rsl, way, g):
        return pltpu.make_async_remote_copy(
            src_ref=src.at[way, g], dst_ref=dst.at[way, g], send_sem=ssem.at[ssl + way * 4 + g],
            recv_sem=rsem.at[rsl + way * 4 + g], device_id=to_tp((xr, xl)[way]),
            device_id_type=pl.DeviceIdType.MESH,
        )

    def hop1(way, g):
        return hop(h1s, h1r, h1_send, h1_base, way, g)

    def hop2(way, g):
        return hop(h2s, h2r, h2_send, h2_base, way, g)

    def pair_sum(k, g):
        pair_copy(k, g).wait_recv()
        for xx in range(4):
            mine[g, xx] += precv[g, xx].astype(F32)
        for way in range(2):
            h1s[way, g] = mine[g, co, way * ROWS : (way + 1) * ROWS, :].astype(BF16)
            hop1(way, g).start()

    def middle(g):
        for way in range(2):
            hop1(way, g).wait_recv()
            dest = (cr, cl)[way]
            near, other = way * ROWS, (1 - way) * ROWS
            h2s[way, g, near : near + ROWS, :] = (
                mine[g, dest, near : near + ROWS, :] + h1r[way, g].astype(F32)
            ).astype(BF16)
            h2s[way, g, other : other + ROWS, :] = mine[g, dest, other : other + ROWS, :].astype(BF16)
            hop2(way, g).start()

    def last(g):
        hop2(0, g).wait_recv()
        hop2(1, g).wait_recv()
        total = mine[g, x] + h2r[0, g].astype(F32) + h2r[1, g].astype(F32)
        key = total[:, :HD]
        r = pl.ds(pl.multiple_of(g * GROUP, GROUP), GROUP)
        place = pl.ds(pl.multiple_of((g % 2) * GROUP, GROUP), GROUP)
        kbuf[r, :] = (key * ktab[0, place, :] + pltpu.roll(key, HD // 2, 1) * ktab[1, place, :]).astype(BF16)
        vt[:, r] = total[:, HD:].T.astype(BF16)

    load1.wait()
    row_ring.mates(0)
    hidden(x)
    y_first.forward()
    z_first.forward()
    row_ring.forward()
    y_first.finish()
    z_first.finish()
    z_then.open()
    y_then.open()
    row_ring.near()
    z_then.forward()
    y_then.forward()
    row_ring.mates(1)
    hidden(cl)
    row_ring.mates(2)
    hidden(cr)
    z_then.finish()
    y_then.finish()
    project(0, x)
    project(1, cl)
    pair_sum(0, x)
    project(2, cr)
    pair_sum(1, cl)
    row_ring.far()
    pair_sum(2, cr)
    row_ring.mates(3)
    hidden(co)
    project(3, co)
    pair_sum(3, co)
    order = (x, cl, cr, co)
    for g in order:
        middle(g)
    for g in order:
        last(g)

    load4.wait()

    @pl.loop(1, NS)
    def _(i):
        q_copy(i).wait_recv()

    inv_root = np.float32(1.0 / math.sqrt(HD))
    cited = [meta[:, j : j + 1] for j in range(CITE)]
    counts, prefill, decode = meta[:, 4:5], meta[:, 5:6], meta[:, 6:7]
    code = jnp.zeros((HD, 1), F32)
    for j in range(CITE):
        hit = (counts > j) & ((cited[j] // 2) == s)
        code += jnp.where(hit, (1 + (cited[j] % 2) + 2 * (counts - 1 - j)).astype(F32), 0.0)
    lane = lax.broadcasted_iota(jnp.int32, (HD, HD), 1)
    sub = lax.broadcasted_iota(jnp.int32, (HD, HD), 0)
    eye = lane == sub
    mine_o = prefill == (lane % NS)

    def heads_down(block):
        return jnp.concatenate([block[:, h * HD : (h + 1) * HD] for h in range(8)], axis=0)

    o_base = recvs.take(NS)
    o_send = sends.take(NS)

    def part_of(d):
        row = jnp.sum(jnp.where(mine_o & (decode == d), code, 0.0), axis=0, keepdims=True)
        col = jnp.sum(jnp.where(eye, row, 0.0), axis=1, keepdims=True)
        cosine, sine = qtab[0, 0:1, :], qtab[1, 0:1, :]
        for p in range(1, CITE):
            now = (col == 1.0 + 2.0 * p) | (col == 2.0 + 2.0 * p)
            cosine = jnp.where(now, qtab[0, p : p + 1, :], cosine)
            sine = jnp.where(now, qtab[1, p : p + 1, :], sine)
        asks = heads_down(qg[d].astype(F32))
        asks = (asks * cosine + pltpu.roll(asks, HD // 2, 1) * sine).astype(BF16)
        scores = lax.dot_general(kbuf[...], asks, (((1,), (1,)), ((), ())), preferred_element_type=F32)
        second = (row == 2.0) | (row == 4.0) | (row == 6.0) | (row == 8.0)
        frame = jnp.where(second, scores[256:], scores[:256]) * inv_root
        top = jnp.max(frame, axis=0, keepdims=True)
        weight = jnp.exp(frame - top)
        total = jnp.sum(weight, axis=0, keepdims=True)
        both = jnp.concatenate([jnp.where(second, 0.0, weight), jnp.where(second, weight, 0.0)], axis=0)
        value = jnp.dot(vt[...], both.astype(BF16), preferred_element_type=F32) / total
        live = row > 0.0
        osend[d, 0:HD, :] = jnp.where(live, value, 0.0).astype(BF16)
        level = jnp.where(live, top + jnp.log(total), -1e30)
        high = level.astype(BF16).astype(F32)
        mid = (level - high).astype(BF16).astype(F32)
        low = level - high - mid
        pad = jnp.zeros((PART - HD - 3, HD), F32)
        osend[d, HD:PART, :] = jnp.concatenate([high, mid, low, pad], axis=0).astype(BF16)

    def part_copy(i):
        d = (s + i) % NS
        return pltpu.make_async_remote_copy(
            src_ref=osend.at[d], dst_ref=orecv.at[s], send_sem=ssem.at[o_send + i],
            recv_sem=rsem.at[o_base + i], device_id=to_section(d), device_id_type=pl.DeviceIdType.MESH,
        )

    @pl.loop(1, NS)
    def _(i):
        part_of((s + i) % NS)
        part_copy(i).start()

    part_of(s)
    keep = pltpu.make_async_copy(osend.at[s], orecv.at[s], lsem.at[4])
    keep.start()

    asks = heads_down(q[...].astype(F32)).astype(BF16)
    own = lax.dot_general(nkv[:, :HD], asks, (((1,), (1,)), ((), ())), preferred_element_type=F32)
    pick = (lax.broadcasted_iota(jnp.int32, (NS, HD), 1) % NS) == lax.broadcasted_iota(jnp.int32, (NS, HD), 0)
    own = jnp.sum(jnp.where(pick, own, 0.0), axis=0, keepdims=True) * inv_root
    value = nkv[:, HD:].astype(F32)
    value = jnp.concatenate([value] * 8, axis=0).T
    present = jnp.sum(jnp.where(mine_o & (decode == s), 1.0, 0.0), axis=0, keepdims=True)

    keep.wait()

    @pl.loop(1, NS)
    def _(i):
        part_copy(i).wait_recv()

    tail = [orecv[j, HD:PART, :].astype(F32) for j in range(NS)]
    level = [v[0:1] + v[1:2] + v[2:3] for v in tail]
    top = own
    for v in level:
        top = jnp.maximum(top, v)
    weight = jnp.exp(own - top)
    total, value = weight, value * weight
    for j in range(NS):
        weight = jnp.exp(level[j] - top)
        total += weight
        value += orecv[j, 0:HD, :].astype(F32) * weight
    value = jnp.where(present > 0.0, value / total, 0.0).T
    for h in range(8):
        out[:, h * HD : (h + 1) * HD] = value[h * NS : (h + 1) * NS, :].astype(BF16)

    for copy in pending:
        copy.wait_send()
    for k, g in enumerate(order):
        pair_copy(k, g).wait_send()
        for way in range(2):
            hop1(way, g).wait_send()
            hop2(way, g).wait_send()

    @pl.loop(1, NS)
    def _(i):
        q_copy(i).wait_send()
        part_copy(i).wait_send()

    assert sends.n <= N_SEND and recvs.n <= N_RECV


def shards(
    patch_states, merge_in, merge_out, kv_weight, queries, new_kv, citations, lengths, prefill_owner, decode_owner
):
    meta = jnp.concatenate(
        [citations, lengths[:, None], prefill_owner[:, None], decode_owner[:, None], decode_owner[:, None]], axis=1
    )
    keys, asks = tables()
    vmem = pl.BlockSpec(memory_space=pltpu.VMEM)
    anywhere = pl.BlockSpec(memory_space=pl.ANY)
    result = pl.pallas_call(
        kernel,
        out_shape=jax.ShapeDtypeStruct((NS, 8 * HD), BF16),
        in_specs=[vmem, anywhere, anywhere, anywhere, vmem, vmem, vmem, vmem, vmem],
        out_specs=vmem,
        scratch_shapes=[
            pltpu.VMEM((TOKENS, KIN), BF16),
            pltpu.VMEM((KIN, HU), BF16),
            pltpu.VMEM((HU, 8192), BF16),
            pltpu.VMEM((8192, HD), BF16),
            pltpu.VMEM((HU, HD), F32),
            pltpu.VMEM((4, 2, HU, 2 * HD), BF16),
            pltpu.VMEM((4, GROUP, HU), F32),
            pltpu.VMEM((4, 4, GROUP, 2 * HD), F32),
            pltpu.VMEM((4, 4, GROUP, 2 * HD), BF16),
            pltpu.VMEM((4, 4, GROUP, 2 * HD), BF16),
            pltpu.VMEM((2, 4, ROWS, 2 * HD), BF16),
            pltpu.VMEM((2, 4, ROWS, 2 * HD), BF16),
            pltpu.VMEM((2, 4, GROUP, 2 * HD), BF16),
            pltpu.VMEM((2, 4, GROUP, 2 * HD), BF16),
            pltpu.VMEM((TOKENS, HD), BF16),
            pltpu.VMEM((8, HD), BF16),
            pltpu.VMEM((HD, TOKENS), BF16),
            pltpu.VMEM((NS, NS, 8 * HD), BF16),
            pltpu.VMEM((NS, PART, HD), BF16),
            pltpu.VMEM((NS, PART, HD), BF16),
            pltpu.SemaphoreType.DMA((N_SEND,)),
            pltpu.SemaphoreType.DMA((N_RECV,)),
            pltpu.SemaphoreType.DMA((N_LOCAL,)),
        ],
        compiler_params=pltpu.CompilerParams(
            collective_id=0, has_side_effects=True, vmem_limit_bytes=58 * 1024 * 1024
        ),
    )(
        patch_states, merge_in, merge_out, kv_weight, queries[0], new_kv[0], meta,
        jnp.asarray(keys), jnp.asarray(asks),
    )
    return result[None]


def solution(mesh):
    return jax.shard_map(
        shards,
        mesh=mesh,
        in_specs=(
            P(("section", "tp"), None),
            P(None, "tp"),
            P("tp", None),
            P("tp", None),
            P("section", None, "tp"),
            P("section", None, "tp"),
            P(),
            P(),
            P(),
            P(),
        ),
        out_specs=P("section", None, "tp"),
        check_vma=False,
    )
```

time: 630 us -> 83.9 us (0.13); the launches traced: 622 us -> 83.7 us
  waiting for transfers between devices: 456 us -> 0 us
  Pallas kernels: 0 us -> 80.9 us
  local copies, waits for them, and re-layouts: 55.4 us -> 2.84 us
  matrix products: 45.1 us -> 0 us
  other arithmetic: 39.1 us -> 0 us
  starting transfers between devices: 13.7 us -> 0 us
  between operations: 13.4 us -> 0.01 us
    all_to_all x2 -> x0, waiting for transfers between devices: 235 us -> none  [the longest x1 120 us: shards(): lax.all_to_all(stacked, 'section', split_axis=0, concat_axis=0, tiled=True)]
    reduce_scatter x2 -> x0, waiting for transfers between devices: 180 us -> none  [the longest x1 90.4 us: shards(): lax.psum_scatter(head_terms(gathered_rows, kv_weight, heads_local * lax.a...]
    pallas_call x0 -> x1, Pallas kernels: none -> 80.9 us  [shards(): pl.pallas_call(kernel, out_shape=jax.ShapeDtypeStruct((NS, 8 * HD), BF16)...]
    dot_general x5 -> x0, matrix products: 45.1 us -> none  [the longest x1 23.5 us: shards(): jnp.dot(hidden, merge_out, preferred_element_type=jnp.float32)]
    all_gather x1 -> x0, waiting for transfers between devices: 40.2 us -> none  [shards(): lax.all_gather(normed, 'tp', axis=0, tiled=True)]
    gather x9 -> x0, local copies, waits for them, and re-layouts: 30.8 us -> none  [the longest x2 17.3 us: shards(): page_table[page_slots.reshape(-1)]]
    concatenate x1 -> x0, other arithmetic: 16.1 us -> none  [rotate_keys(): jnp.concatenate([first_half * cosine - second_half * sine_part, second_ha...]
    all_to_all x2 -> x0, starting transfers between devices: 13.5 us -> none  [the longest x1 6.84 us: shards(): lax.all_to_all(stacked, 'section', split_axis=0, concat_axis=0, tiled=True)]
  transfers between devices with their start and end apart: 5 -> 0, of which waited for: 5 -> 0; matrix products, arithmetic and copies ran while one was open for 2% -> 0% of each run, Pallas kernels for 0% -> 0%
where the time goes in v1:
time: 83.9 us; the launch traced here: 83.7 us
  Pallas kernels  80.9 us (96%)
  local copies, waits for them, and re-layouts  2.84 us (3%)
    pallas_call x1, Pallas kernels, shards(): pl.pallas_call(kernel, out_shape=jax.ShapeDtypeStruct((NS, 8 * HD), BF16)...  80.9 us

profile of v1, /device:TPU:1, one launch (start us, length us, event | category | flops | bytes accessed | tf_op | source)
XLA Modules:
  0.0 83.7 jit_solution(1677966577813123085)
XLA Ops:
  0.0 0.7 concatenate.3
  0.7 0.7 copy.18.meta
  1.5 80.9 %shard_map.118 = bf16[16,1024]{1,0:T(8,128)(2,1)} custom-call(bf16[64,5120]{1,0:T(8,128)(2,1)} %patch.1, bf16[5120,640]{1,0:T(8,128)(2,1)} %w1.1, bf16[640,8192]{1,0:T(8,128)(2,1)} %w2.1, bf16[1024,2048]{1,0:T(8,128)(2,1)} %kvw.1, bf16[16,1024]{1,0:T(8,128)(2,1)} %bitcast.7, bf16[16,256]{1,0:T(8,128)(2,1)} %bitcast.8, s32[128,8]{1,0:T(8,128)} %copy.18.meta, ...), custom_call_target="tpu_custom_call" | custom-call | tf_op jit(solution)/shard_map/pallas_call | solution.py:516
  82.3 1.4 %copy.20 = bf16[1,16,1024]{2,1,0:T(8,128)(2,1)} copy(bf16[1,16,1024]{2,1,0:T(8,128)(2,1)} %bitcast.6) | data formatting | bytes 65536

commit v2 on v1

v2 whole, which is shorter than its diff:
```python
import math

import jax
import jax.numpy as jnp
import numpy as np
from jax import lax
from jax.experimental import pallas as pl
from jax.experimental.pallas import tpu as pltpu
from jax.sharding import PartitionSpec as P

F32 = jnp.float32
BF16 = jnp.bfloat16
VIT = 1280
HD = 128
GRID = 16
NS = 16
CITE = 4
ROWS = 64
GROUP = 128
TOKENS = 512
KIN = 5120
HU = 640
KVB = 1024
HALF = HU // 2
QUARTER = HU // 4
PART = 144


def tables():
    slot = np.arange(HD // 2)
    inverse = np.exp(slot.astype(np.float32) * np.float32(-2.0 * math.log(1000000.0) / HD)).astype(np.float32)
    token = np.arange(GRID * GRID)
    height = (token // GRID).astype(np.float32)
    across = (token % GRID).astype(np.float32)
    first = HD // 8
    second = first + 3 * HD // 16
    spatial = np.where(slot[None, :] < second, height[:, None], across[:, None])
    spatial = np.where(slot[None, :] < first, np.float32(0.0), spatial) * inverse[None, :]
    cosine, sine = np.cos(spatial), np.sin(spatial)
    keys = np.stack([np.concatenate([cosine, cosine], 1), np.concatenate([-sine, sine], 1)])
    steps = np.arange(CITE).astype(np.float32)[:, None] * inverse[None, :]
    steps = np.where(slot[None, :] < first, steps, np.float32(0.0))
    cosine, sine = np.cos(steps), np.sin(steps)
    asks = np.stack([np.concatenate([cosine, cosine], 1), np.concatenate([sine, -sine], 1)])
    return keys.astype(np.float32), asks.astype(np.float32)


class Counter:
    def __init__(self):
        self.n = 0

    def take(self, k=1):
        first = self.n
        self.n += k
        return first


N_SEND = 104
N_RECV = 104
N_LOCAL = 8


def kernel(
    patch, w1, w2, kvw, q, nkv, cites, lens, prefills, decodes, ktab, qtab, out,
    rows, w1v, w2v, kvg, wacc, wg, hacc, hidb, mine, psend, precv, h1s, h1r, h2s, h2r,
    kbuf, vt, qg, askb, codeb, osend, orecv, ssem, rsem, lsem,
):
    s = lax.axis_index("section")
    t = lax.axis_index("tp")
    x, c = t // 2, t % 2
    z, y = s // 4, s % 4
    mate = 2 * x + (1 - c)
    cr, cl, co = (x + 1) % 4, (x + 3) % 4, (x + 2) % 4
    xr, xl, xo = 2 * cr + c, 2 * cl + c, 2 * co + c
    yn, yp, yo = (y + 1) % 4, (y + 3) % 4, (y + 2) % 4
    zn, zp, zo = (z + 1) % 4, (z + 3) % 4, (z + 2) % 4
    sends, recvs = Counter(), Counter()
    pending = []

    def to_tp(who):
        return {"tp": who}

    def to_section(who):
        return {"section": who}

    def start(src, dst, slot, dev):
        copy = pltpu.make_async_remote_copy(
            src_ref=src, dst_ref=dst, send_sem=ssem.at[sends.take()], recv_sem=rsem.at[slot],
            device_id=dev, device_id_type=pl.DeviceIdType.MESH,
        )
        copy.start()
        pending.append(copy)

    def arrive(dst, slot):
        pltpu.make_async_remote_copy(
            src_ref=dst, dst_ref=dst, send_sem=ssem.at[0], recv_sem=rsem.at[slot],
            device_id=to_tp(mate), device_id_type=pl.DeviceIdType.MESH,
        ).wait_recv()

    load1 = pltpu.make_async_copy(w1, w1v, lsem.at[0])
    load2 = pltpu.make_async_copy(w2, w2v, lsem.at[1])
    cols = pl.ds(pl.multiple_of(s * HD, HD), HD)

    def kv_at(b, h=None):
        if h is None:
            return kvg.at[pl.ds(pl.multiple_of(b * KVB, KVB), KVB), :]
        return kvg.at[pl.ds(pl.multiple_of(b * KVB + h * (KVB // 2), KVB // 2), KVB // 2), :]

    def rows_at(b, h=None):
        if h is None:
            return rows.at[pl.ds(pl.multiple_of(b * ROWS, ROWS), ROWS), :]
        return rows.at[pl.ds(pl.multiple_of(b * ROWS + h * (ROWS // 2), ROWS // 2), ROWS // 2), :]

    load3 = pltpu.make_async_copy(kvw.at[:, cols], kv_at(t), lsem.at[2])
    load4 = pltpu.make_async_copy(q, qg.at[z, y], lsem.at[3])
    load3.start()
    load4.start()
    load2.start()
    load1.start()

    def sec(zz, yy):
        return to_section(zz * 4 + yy)

    barrier = pltpu.get_barrier_semaphore()
    neighbours = (to_tp(mate), to_tp(xr), to_tp(xl), sec(z, yn), sec(z, yp), sec(zn, y), sec(zp, y))
    for who in neighbours:
        pl.semaphore_signal(barrier, inc=1, device_id=who, device_id_type=pl.DeviceIdType.MESH)

    for b in range(KIN // VIT):
        span = pl.ds(b * VIT, VIT)
        block = patch[:, span].astype(F32)
        centered = block - jnp.mean(block, axis=-1, keepdims=True)
        variance = jnp.mean(centered * centered, axis=-1, keepdims=True)
        rows[pl.ds(pl.multiple_of(t * ROWS, ROWS), ROWS), span] = (
            centered * lax.rsqrt(variance + 1e-06)
        ).astype(BF16)

    load3.wait()
    load4.wait()
    pl.semaphore_wait(barrier, len(neighbours))

    class Ring:
        def __init__(self, at):
            self.at = at
            self.base = recvs.take(10)

        def open(self, own):
            b = self.base
            start(own(0), self.at(t, 0), b + 0, to_tp(xr))
            start(own(1), self.at(t, 1), b + 3, to_tp(xl))
            start(own(1), self.at(t, 1), b + 1, to_tp(xr))
            start(own(0), self.at(t, 0), b + 2, to_tp(xl))
            start(own(None), self.at(t), b + 6, to_tp(mate))

        def forward(self):
            b = self.base
            arrive(self.at(xl, 0), b + 0)
            start(self.at(xl, 0), self.at(xl, 0), b + 4, to_tp(xr))
            arrive(self.at(xr, 1), b + 3)
            start(self.at(xr, 1), self.at(xr, 1), b + 5, to_tp(xl))

        def near(self):
            b = self.base
            arrive(self.at(xl, 1), b + 1)
            start(self.at(xl), self.at(xl), b + 7, to_tp(mate))
            arrive(self.at(xr, 0), b + 2)
            start(self.at(xr), self.at(xr), b + 8, to_tp(mate))

        def far(self):
            b = self.base
            arrive(self.at(xo, 0), b + 4)
            arrive(self.at(xo, 1), b + 5)
            start(self.at(xo), self.at(xo), b + 9, to_tp(mate))

        def mates(self, k):
            chip = (x, cl, cr, co)[k]
            arrive(self.at(2 * chip + (1 - c)), self.base + 6 + k)

    kv_ring = Ring(kv_at)
    kv_ring.open(lambda h: kv_at(t, h))

    class Cross:
        def __init__(self, at, me, nxt, prv, opp, dev_n, dev_p, r0, half):
            self.at, self.me, self.nxt, self.prv, self.opp = at, me, nxt, prv, opp
            self.dev_n, self.dev_p, self.r0, self.half = dev_n, dev_p, r0, half
            self.base = recvs.take(6)

        def low(self, k):
            return self.at(k, self.r0, self.half // 2)

        def high(self, k):
            return self.at(k, self.r0 + self.half // 2, self.half // 2)

        def open(self):
            b, low, high = self.base, self.low(self.me), self.high(self.me)
            start(low, low, b + 0, self.dev_n)
            start(high, high, b + 3, self.dev_p)
            start(high, high, b + 1, self.dev_n)
            start(low, low, b + 2, self.dev_p)

        def forward(self):
            b, low, high = self.base, self.low(self.prv), self.high(self.nxt)
            arrive(low, b + 0)
            start(low, low, b + 4, self.dev_n)
            arrive(high, b + 3)
            start(high, high, b + 5, self.dev_p)

        def finish(self):
            b = self.base
            arrive(self.high(self.prv), b + 1)
            arrive(self.low(self.nxt), b + 2)
            arrive(self.low(self.opp), b + 4)
            arrive(self.high(self.opp), b + 5)

    to_y = (y, yn, yp, yo, sec(z, yn), sec(z, yp))
    to_z = (z, zn, zp, zo, sec(zn, y), sec(zp, y))

    qy_first = Cross(lambda yy, r, n: qg.at[z, yy, :, pl.ds(r, n)], *to_y, 0, 512)
    qz_first = Cross(lambda zz, r, n: qg.at[zz, y, :, pl.ds(r, n)], *to_z, 512, 512)
    qz_then = Cross(lambda zz, r, n: qg.at[zz, :, :, pl.ds(r, n)], *to_z, 0, 512)
    qy_then = Cross(lambda yy, r, n: qg.at[:, yy, :, pl.ds(r, n)], *to_y, 512, 512)
    qy_first.open()
    qz_first.open()

    def w_step(b, first=False):
        part = jnp.dot(
            w2v[:, pl.ds(pl.multiple_of(b * KVB, KVB), KVB)],
            kvg[pl.ds(pl.multiple_of(b * KVB, KVB), KVB), :],
            preferred_element_type=F32,
        )
        if first:
            wacc[...] = part
        else:
            wacc[...] += part

    load2.wait()
    w_step(t, first=True)
    kv_ring.mates(0)
    w_step(mate)
    kv_ring.forward()
    row_ring = Ring(rows_at)
    row_ring.open(lambda h: rows_at(t, h))
    qy_first.forward()
    qz_first.forward()
    kv_ring.near()
    w_step(xl)
    w_step(xr)
    kv_ring.mates(1)
    w_step(2 * cl + (1 - c))
    kv_ring.mates(2)
    w_step(2 * cr + (1 - c))
    qy_first.finish()
    qz_first.finish()
    qz_then.open()
    qy_then.open()
    kv_ring.far()
    w_step(xo)
    kv_ring.mates(3)
    w_step(2 * co + (1 - c))

    def lanes(yy):
        return pl.ds(pl.multiple_of((yy % 2) * HD, HD), HD)

    def block_at(zz, yy, r0, n):
        return wg.at[zz, yy // 2, pl.ds(r0, n), lanes(yy)]

    def line_at(zz, r0, n):
        return wg.at[zz, :, pl.ds(r0, n), :]

    def column_at(yy, r0, n):
        return wg.at[:, yy // 2, pl.ds(r0, n), lanes(yy)]

    wg[z, y // 2, :, lanes(y)] = wacc[...].astype(BF16)

    y_first = Cross(lambda yy, r, n: block_at(z, yy, r, n), *to_y, 0, HALF)
    z_first = Cross(lambda zz, r, n: block_at(zz, y, r, n), *to_z, HALF, HALF)
    z_then = Cross(line_at, *to_z, 0, HALF)
    y_then = Cross(column_at, *to_y, HALF, HALF)
    y_first.open()
    z_first.open()

    def hidden(g):
        r = pl.ds(pl.multiple_of(g * GROUP, GROUP), GROUP)

        def part(k):
            span = pl.ds(pl.multiple_of(k * 1024, 1024), 1024)
            return jnp.dot(rows[r, span], w1v[span, :], preferred_element_type=F32)

        hacc[...] = part(0)

        @pl.loop(1, KIN // 1024)
        def _(k):
            hacc[...] += part(k)

        pre = hacc[...]
        hidb[g] = (0.5 * pre * (1.0 + lax.erf(pre * np.float32(math.sqrt(0.5))))).astype(BF16)

    p_base = recvs.take(4)
    p_send = sends.take(4)

    def pair_copy(k, g):
        return pltpu.make_async_remote_copy(
            src_ref=psend.at[g], dst_ref=precv.at[g], send_sem=ssem.at[p_send + k],
            recv_sem=rsem.at[p_base + k], device_id=to_tp(mate), device_id_type=pl.DeviceIdType.MESH,
        )

    def project(k, g):
        hid = hidb[g]
        for xx in range(4):
            psend[g, xx] = jnp.dot(hid, wg[xx, 1 - c], preferred_element_type=F32).astype(BF16)
        pair_copy(k, g).start()
        for xx in range(4):
            mine[g, xx] = jnp.dot(hid, wg[xx, c], preferred_element_type=F32)

    h1_base = recvs.take(8)
    h1_send = sends.take(8)
    h2_base = recvs.take(8)
    h2_send = sends.take(8)

    def hop(src, dst, ssl, rsl, way, g):
        return pltpu.make_async_remote_copy(
            src_ref=src.at[way, g], dst_ref=dst.at[way, g], send_sem=ssem.at[ssl + way * 4 + g],
            recv_sem=rsem.at[rsl + way * 4 + g], device_id=to_tp((xr, xl)[way]),
            device_id_type=pl.DeviceIdType.MESH,
        )

    def hop1(way, g):
        return hop(h1s, h1r, h1_send, h1_base, way, g)

    def hop2(way, g):
        return hop(h2s, h2r, h2_send, h2_base, way, g)

    def pair_sum(k, g):
        pair_copy(k, g).wait_recv()
        for xx in range(4):
            mine[g, xx] += precv[g, xx].astype(F32)
        for way in range(2):
            h1s[way, g] = mine[g, co, way * ROWS : (way + 1) * ROWS, :].astype(BF16)
            hop1(way, g).start()

    def middle(way, g):
        hop1(way, g).wait_recv()
        dest = (cr, cl)[way]
        near, other = way * ROWS, (1 - way) * ROWS
        h2s[way, g, near : near + ROWS, :] = (
            mine[g, dest, near : near + ROWS, :] + h1r[way, g].astype(F32)
        ).astype(BF16)
        h2s[way, g, other : other + ROWS, :] = mine[g, dest, other : other + ROWS, :].astype(BF16)
        hop2(way, g).start()

    def last(g):
        hop2(0, g).wait_recv()
        hop2(1, g).wait_recv()
        total = mine[g, x] + h2r[0, g].astype(F32) + h2r[1, g].astype(F32)
        key = total[:, :HD]
        r = pl.ds(pl.multiple_of(g * GROUP, GROUP), GROUP)
        place = pl.ds(pl.multiple_of((g % 2) * GROUP, GROUP), GROUP)
        kbuf[r, :] = (key * ktab[0, place, :] + pltpu.roll(key, HD // 2, 1) * ktab[1, place, :]).astype(BF16)
        vt[:, r] = total[:, HD:].T.astype(BF16)

    lane = lax.broadcasted_iota(jnp.int32, (HD, HD), 1)
    sub = lax.broadcasted_iota(jnp.int32, (HD, HD), 0)
    eye = lane == sub

    def column(row):
        return jnp.sum(jnp.where(eye, row.astype(F32), 0.0), axis=1, keepdims=True)

    def heads_down(block):
        return jnp.concatenate([block[:, h * HD : (h + 1) * HD] for h in range(8)], axis=0)

    def prepare():
        counts = lens[...]
        code = jnp.zeros((1, HD), jnp.int32)
        for j in range(CITE):
            cited = cites[j : j + 1, :]
            hit = (counts > j) & ((cited // 2) == s)
            code += jnp.where(hit, 1 + (cited % 2) + 2 * (counts - 1 - j), 0)
        code = column(code)
        owned = column(prefills[...]) == (lane % NS).astype(F32)
        decode = column(decodes[...])
        codeb[NS] = jnp.sum(
            jnp.where(owned & (decode == s.astype(F32)), 1.0, 0.0), axis=0, keepdims=True
        )

        @pl.loop(0, NS)
        def _(i):
            d = (s + i) % NS
            row = jnp.sum(jnp.where(owned & (decode == d.astype(F32)), code, 0.0), axis=0, keepdims=True)
            codeb[i] = row
            col = column(row)
            cosine, sine = qtab[0, 0:1, :], qtab[1, 0:1, :]
            for p in range(1, CITE):
                now = (col == 1.0 + 2.0 * p) | (col == 2.0 + 2.0 * p)
                cosine = jnp.where(now, qtab[0, p : p + 1, :], cosine)
                sine = jnp.where(now, qtab[1, p : p + 1, :], sine)
            asks = heads_down(qg[d // 4, d % 4].astype(F32))
            askb[i] = (asks * cosine + pltpu.roll(asks, HD // 2, 1) * sine).astype(BF16)

    load1.wait()
    row_ring.mates(0)
    hidden(x)
    y_first.forward()
    z_first.forward()
    qz_then.forward()
    qy_then.forward()
    row_ring.forward()
    y_first.finish()
    z_first.finish()
    z_then.open()
    y_then.open()
    qz_then.finish()
    qy_then.finish()
    prepare()
    z_then.forward()
    y_then.forward()
    row_ring.near()
    row_ring.mates(1)
    hidden(cl)
    row_ring.mates(2)
    hidden(cr)
    z_then.finish()
    y_then.finish()
    project(0, x)
    project(1, cl)
    pair_sum(0, x)
    project(2, cr)
    pair_sum(1, cl)
    row_ring.far()
    pair_sum(2, cr)
    row_ring.mates(3)
    hidden(co)
    middle(0, x)
    middle(1, x)
    middle(0, cl)
    middle(1, cr)
    project(3, co)
    pair_sum(3, co)
    middle(0, cr)
    middle(1, cl)
    middle(0, co)
    middle(1, co)
    order = (x, cl, cr, co)
    for g in order:
        last(g)

    inv_root = np.float32(1.0 / math.sqrt(HD))
    o_base = recvs.take(NS)
    o_send = sends.take(NS)

    def part_of(i):
        asks = askb[pl.ds(i, 2)].reshape(2 * HD, HD)
        row = jnp.concatenate([codeb[i], codeb[i + 1]], axis=1)
        scores = lax.dot_general(kbuf[...], asks, (((1,), (1,)), ((), ())), preferred_element_type=F32)
        second = (row == 2.0) | (row == 4.0) | (row == 6.0) | (row == 8.0)
        frame = jnp.where(second, scores[256:], scores[:256]) * inv_root
        top = jnp.max(frame, axis=0, keepdims=True)
        weight = jnp.exp(frame - top)
        total = jnp.sum(weight, axis=0, keepdims=True)
        both = jnp.concatenate([jnp.where(second, 0.0, weight), jnp.where(second, weight, 0.0)], axis=0)
        value = jnp.dot(vt[...], both.astype(BF16), preferred_element_type=F32) / total
        live = row > 0.0
        value = jnp.where(live, value, 0.0).astype(BF16)
        level = jnp.where(live, top + jnp.log(total), -1e30)
        high = level.astype(BF16).astype(F32)
        mid = (level - high).astype(BF16).astype(F32)
        low = level - high - mid
        pad = jnp.zeros((PART - HD - 3, 2 * HD), F32)
        level = jnp.concatenate([high, mid, low, pad], axis=0).astype(BF16)
        for k in range(2):
            d = (s + i + k) % NS
            osend[d, 0:HD, :] = value[:, k * HD : (k + 1) * HD]
            osend[d, HD:PART, :] = level[:, k * HD : (k + 1) * HD]

    def part_copy(i):
        d = (s + i) % NS
        return pltpu.make_async_remote_copy(
            src_ref=osend.at[d], dst_ref=orecv.at[s], send_sem=ssem.at[o_send + i],
            recv_sem=rsem.at[o_base + i], device_id=to_section(d), device_id_type=pl.DeviceIdType.MESH,
        )

    @pl.loop(1, NS // 2)
    def _(i):
        part_of(2 * i)
        part_copy(2 * i).start()
        part_copy(2 * i + 1).start()

    part_of(0)
    part_copy(1).start()
    keep = pltpu.make_async_copy(osend.at[s], orecv.at[s], lsem.at[4])
    keep.start()

    asks = heads_down(q[...].astype(F32)).astype(BF16)
    own = lax.dot_general(nkv[:, :HD], asks, (((1,), (1,)), ((), ())), preferred_element_type=F32)
    pick = (lax.broadcasted_iota(jnp.int32, (NS, HD), 1) % NS) == lax.broadcasted_iota(jnp.int32, (NS, HD), 0)
    own = jnp.sum(jnp.where(pick, own, 0.0), axis=0, keepdims=True) * inv_root
    value = nkv[:, HD:].astype(F32)
    value = jnp.concatenate([value] * 8, axis=0).T
    present = codeb[NS]

    keep.wait()

    @pl.loop(1, NS)
    def _(i):
        part_copy(i).wait_recv()

    tail = [orecv[j, HD:PART, :].astype(F32) for j in range(NS)]
    level = [v[0:1] + v[1:2] + v[2:3] for v in tail]
    top = own
    for v in level:
        top = jnp.maximum(top, v)
    weight = jnp.exp(own - top)
    total, value = weight, value * weight
    for j in range(NS):
        weight = jnp.exp(level[j] - top)
        total += weight
        value += orecv[j, 0:HD, :].astype(F32) * weight
    value = jnp.where(present > 0.0, value / total, 0.0).T
    for h in range(8):
        out[:, h * HD : (h + 1) * HD] = value[h * NS : (h + 1) * NS, :].astype(BF16)

    for copy in pending:
        copy.wait_send()
    for k, g in enumerate(order):
        pair_copy(k, g).wait_send()
        for way in range(2):
            hop1(way, g).wait_send()
            hop2(way, g).wait_send()

    @pl.loop(1, NS)
    def _(i):
        part_copy(i).wait_send()

    assert (sends.n, recvs.n) == (N_SEND, N_RECV), (sends.n, recvs.n)


def shards(
    patch_states, merge_in, merge_out, kv_weight, queries, new_kv, citations, lengths, prefill_owner, decode_owner
):
    along = (1, citations.shape[0])
    keys, asks = tables()
    vmem = pl.BlockSpec(memory_space=pltpu.VMEM)
    anywhere = pl.BlockSpec(memory_space=pl.ANY)
    result = pl.pallas_call(
        kernel,
        out_shape=jax.ShapeDtypeStruct((NS, 8 * HD), BF16),
        in_specs=[vmem, anywhere, anywhere, anywhere] + [vmem] * 8,
        out_specs=vmem,
        scratch_shapes=[
            pltpu.VMEM((TOKENS, KIN), BF16),
            pltpu.VMEM((KIN, HU), BF16),
            pltpu.VMEM((HU, 8192), BF16),
            pltpu.VMEM((8192, HD), BF16),
            pltpu.VMEM((HU, HD), F32),
            pltpu.VMEM((4, 2, HU, 2 * HD), BF16),
            pltpu.VMEM((GROUP, HU), F32),
            pltpu.VMEM((4, GROUP, HU), BF16),
            pltpu.VMEM((4, 4, GROUP, 2 * HD), F32),
            pltpu.VMEM((4, 4, GROUP, 2 * HD), BF16),
            pltpu.VMEM((4, 4, GROUP, 2 * HD), BF16),
            pltpu.VMEM((2, 4, ROWS, 2 * HD), BF16),
            pltpu.VMEM((2, 4, ROWS, 2 * HD), BF16),
            pltpu.VMEM((2, 4, GROUP, 2 * HD), BF16),
            pltpu.VMEM((2, 4, GROUP, 2 * HD), BF16),
            pltpu.VMEM((TOKENS, HD), BF16),
            pltpu.VMEM((HD, TOKENS), BF16),
            pltpu.VMEM((4, 4, NS, 8 * HD), BF16),
            pltpu.VMEM((NS, HD, HD), BF16),
            pltpu.VMEM((NS + 1, 1, HD), F32),
            pltpu.VMEM((NS, PART, HD), BF16),
            pltpu.VMEM((NS, PART, HD), BF16),
            pltpu.SemaphoreType.DMA((N_SEND,)),
            pltpu.SemaphoreType.DMA((N_RECV,)),
            pltpu.SemaphoreType.DMA((N_LOCAL,)),
        ],
        compiler_params=pltpu.CompilerParams(
            collective_id=0, has_side_effects=True, vmem_limit_bytes=58 * 1024 * 1024
        ),
    )(
        patch_states, merge_in, merge_out, kv_weight, queries[0], new_kv[0],
        citations.T, lengths.reshape(along), prefill_owner.reshape(along), decode_owner.reshape(along),
        jnp.asarray(keys), jnp.asarray(asks),
    )
    return result[None]


def solution(mesh):
    return jax.shard_map(
        shards,
        mesh=mesh,
        in_specs=(
            P(("section", "tp"), None),
            P(None, "tp"),
            P("tp", None),
            P("tp", None),
            P("section", None, "tp"),
            P("section", None, "tp"),
            P(),
            P(),
            P(),
            P(),
        ),
        out_specs=P("section", None, "tp"),
        check_vma=False,
    )
```

time: 83.9 us -> 73.3 us (0.87)
  Pallas kernels: 80.9 us -> 71.7 us
  local copies, waits for them, and re-layouts: 2.84 us -> 1.38 us
    pallas_call x1, Pallas kernels: 80.9 us -> 71.7 us  [shards(): pl.pallas_call(kernel, out_shape=jax.ShapeDtypeStruct((NS, 8 * HD), BF16)...]
    concatenate x2 -> x0, local copies, waits for them, and re-layouts: 1.47 us -> none  [shards(): jnp.concatenate([citations, lengths[:, None], prefill_owner[:, None], dec...]
where the time goes in v2:
time: 73.3 us; the launch traced here: 73.1 us
  Pallas kernels  71.7 us (98%)
  local copies, waits for them, and re-layouts  1.38 us (2%)
    pallas_call x1, Pallas kernels, shards(): pl.pallas_call(kernel, out_shape=jax.ShapeDtypeStruct((NS, 8 * HD), BF16)...  71.7 us

profile of v2, /device:TPU:1, one launch (start us, length us, event | category | flops | bytes accessed | tf_op | source)
XLA Modules:
  0.0 73.1 jit_solution(1242427320685110238)
XLA Ops:
  0.0 71.7 %shard_map.118 = bf16[16,1024]{1,0:T(8,128)(2,1)} custom-call(bf16[64,5120]{1,0:T(8,128)(2,1)} %patch.1, bf16[5120,640]{1,0:T(8,128)(2,1)} %w1.1, bf16[640,8192]{1,0:T(8,128)(2,1)} %w2.1, bf16[1024,2048]{1,0:T(8,128)(2,1)} %kvw.1, bf16[16,1024]{1,0:T(8,128)(2,1)} %bitcast.8, bf16[16,256]{1,0:T(8,128)(2,1)} %bitcast.9, s32[4,128]{1,0:T(4,128)} %bitcast.10, ...), custom_call_target="tpu_custom_call" | custom-call | tf_op jit(solution)/shard_map/pallas_call | solution.py:543
  71.7 1.4 %copy.14 = bf16[1,16,1024]{2,1,0:T(8,128)(2,1)} copy(bf16[1,16,1024]{2,1,0:T(8,128)(2,1)} %bitcast.7) | data formatting | bytes 65536

commit v3 on v1

v3 whole, which is shorter than its diff:
```python
import math

import jax
import jax.numpy as jnp
import numpy as np
from jax import lax
from jax.experimental import pallas as pl
from jax.experimental.pallas import tpu as pltpu
from jax.sharding import PartitionSpec as P

F32 = jnp.float32
BF16 = jnp.bfloat16
VIT = 1280
HD = 128
GRID = 16
NS = 16
CITE = 4
ROWS = 64
GROUP = 128
TOKENS = 512
KIN = 5120
HU = 640
CHUNK = 1024
KVB = 1024
HALF = HU // 2
QUARTER = HU // 4


def tables():
    slot = np.arange(HD // 2)
    inverse = np.exp(slot.astype(np.float32) * np.float32(-2.0 * math.log(1000000.0) / HD)).astype(np.float32)
    token = np.arange(GRID * GRID)
    height = (token // GRID).astype(np.float32)
    across = (token % GRID).astype(np.float32)
    first = HD // 8
    second = first + 3 * HD // 16
    spatial = np.where(slot[None, :] < second, height[:, None], across[:, None])
    spatial = np.where(slot[None, :] < first, np.float32(0.0), spatial) * inverse[None, :]
    cosine, sine = np.cos(spatial), np.sin(spatial)
    keys = np.stack([np.concatenate([cosine, cosine], 1), np.concatenate([-sine, sine], 1)])
    steps = np.arange(CITE).astype(np.float32)[:, None] * inverse[None, :]
    steps = np.where(slot[None, :] < first, steps, np.float32(0.0))
    cosine, sine = np.cos(steps), np.sin(steps)
    asks = np.stack([np.concatenate([cosine, cosine], 1), np.concatenate([sine, -sine], 1)])
    return keys.astype(np.float32), asks.astype(np.float32)


class Counter:
    def __init__(self):
        self.n = 0

    def take(self, k=1):
        first = self.n
        self.n += k
        return first


N_SEND = 10
N_RECV = 110
N_LOCAL = 7


def kernel(
    patch_in, w1, w2, kvw, q, nkv, cites, lens, prefills, decodes, ktab_in, qtab, out,
    patch, ktab, rows, w1v, w2v, kvg, wacc, wg, hacc, hidb, mine, psend, precv, gsend, grecv,
    kbuf, vt, qg, askb, codeb, osend, orecv, lsend, lrecv, ssem, rsem, lsem,
):
    s = lax.axis_index("section")
    t = lax.axis_index("tp")
    x, c = t // 2, t % 2
    z, y = s // 4, s % 4
    mate = 2 * x + (1 - c)
    cr, cl, co = (x + 1) % 4, (x + 3) % 4, (x + 2) % 4
    xr, xl, xo = 2 * cr + c, 2 * cl + c, 2 * co + c
    yn, yp, yo = (y + 1) % 4, (y + 3) % 4, (y + 2) % 4
    zn, zp, zo = (z + 1) % 4, (z + 3) % 4, (z + 2) % 4
    recvs = Counter()
    kv_out, row_out, q_out, q_out_then, a_out, b_out, p_out, g_out, o_out, l_out = range(10)

    def to_tp(who):
        return {"tp": who}

    def to_section(who):
        return {"section": who}

    def remote(src, dst, kind, slot, dev):
        return pltpu.make_async_remote_copy(
            src_ref=src, dst_ref=dst, send_sem=ssem.at[kind], recv_sem=rsem.at[slot],
            device_id=dev, device_id_type=pl.DeviceIdType.MESH,
        )

    def start(src, dst, kind, slot, dev):
        remote(src, dst, kind, slot, dev).start()

    def arrive(dst, slot):
        remote(dst, dst, 0, slot, to_tp(mate)).wait_recv()

    def sent(kind, ref):
        remote(ref, ref, kind, 0, to_tp(mate)).wait_send()

    def sec(zz, yy):
        return to_section(zz * 4 + yy)

    barrier = pltpu.get_barrier_semaphore()
    neighbours = (to_tp(mate), to_tp(xr), to_tp(xl), sec(z, yn), sec(z, yp), sec(zn, y), sec(zp, y))
    for who in neighbours:
        pl.semaphore_signal(barrier, inc=1, device_id=who, device_id_type=pl.DeviceIdType.MESH)

    load1 = pltpu.make_async_copy(w1, w1v, lsem.at[0])
    load2 = pltpu.make_async_copy(w2, w2v, lsem.at[1])
    cols = pl.ds(pl.multiple_of(s * HD, HD), HD)

    def kv_at(b, h=None):
        if h is None:
            return kvg.at[pl.ds(pl.multiple_of(b * KVB, KVB), KVB), :]
        return kvg.at[pl.ds(pl.multiple_of(b * KVB + h * (KVB // 2), KVB // 2), KVB // 2), :]

    def rows_at(b, h=None):
        if h is None:
            return rows.at[pl.ds(pl.multiple_of(b * ROWS, ROWS), ROWS), :]
        return rows.at[pl.ds(pl.multiple_of(b * ROWS + h * (ROWS // 2), ROWS // 2), ROWS // 2), :]

    load3 = pltpu.make_async_copy(kvw.at[:, cols], kv_at(t), lsem.at[2])
    load4 = pltpu.make_async_copy(q, qg.at[z, y], lsem.at[3])
    load5 = pltpu.make_async_copy(patch_in, patch, lsem.at[5])
    load6 = pltpu.make_async_copy(ktab_in, ktab, lsem.at[6])
    load3.start()
    load4.start()
    load5.start()
    load2.start()
    load1.start()
    load6.start()

    load3.wait()
    pl.semaphore_wait(barrier, len(neighbours))

    class Ring:
        def __init__(self, at, kind):
            self.at, self.kind = at, kind
            self.base = recvs.take(10)

        def go(self, *rest):
            start(*rest[:2], self.kind, *rest[2:])

        def open(self, own):
            b = self.base
            self.go(own(0), self.at(t, 0), b + 0, to_tp(xr))
            self.go(own(1), self.at(t, 1), b + 3, to_tp(xl))
            self.go(own(1), self.at(t, 1), b + 1, to_tp(xr))
            self.go(own(0), self.at(t, 0), b + 2, to_tp(xl))
            self.go(own(None), self.at(t), b + 6, to_tp(mate))

        def forward(self):
            b = self.base
            arrive(self.at(xl, 0), b + 0)
            self.go(self.at(xl, 0), self.at(xl, 0), b + 4, to_tp(xr))
            arrive(self.at(xr, 1), b + 3)
            self.go(self.at(xr, 1), self.at(xr, 1), b + 5, to_tp(xl))

        def near(self):
            b = self.base
            arrive(self.at(xl, 1), b + 1)
            self.go(self.at(xl), self.at(xl), b + 7, to_tp(mate))
            arrive(self.at(xr, 0), b + 2)
            self.go(self.at(xr), self.at(xr), b + 8, to_tp(mate))

        def far(self):
            b = self.base
            arrive(self.at(xo, 0), b + 4)
            arrive(self.at(xo, 1), b + 5)
            self.go(self.at(xo), self.at(xo), b + 9, to_tp(mate))

        def mates(self, k):
            chip = (x, cl, cr, co)[k]
            arrive(self.at(2 * chip + (1 - c)), self.base + 6 + k)

    kv_ring = Ring(kv_at, kv_out)
    kv_ring.open(lambda h: kv_at(t, h))

    class Cross:
        def __init__(self, at, me, nxt, prv, opp, dev_n, dev_p, r0, half, kind):
            self.at, self.me, self.nxt, self.prv, self.opp = at, me, nxt, prv, opp
            self.dev_n, self.dev_p, self.r0, self.half, self.kind = dev_n, dev_p, r0, half, kind
            self.base = recvs.take(4)

        def low(self, k):
            return self.at(k, self.r0, self.half // 2)

        def high(self, k):
            return self.at(k, self.r0 + self.half // 2, self.half // 2)

        def open(self):
            own = self.at(self.me, self.r0, self.half)
            start(own, own, self.kind, self.base, self.dev_n)
            start(own, own, self.kind, self.base + 1, self.dev_p)

        def forward(self):
            b, low, high = self.base, self.low(self.prv), self.high(self.nxt)
            arrive(self.at(self.prv, self.r0, self.half), b)
            start(low, low, self.kind, b + 2, self.dev_n)
            arrive(self.at(self.nxt, self.r0, self.half), b + 1)
            start(high, high, self.kind, b + 3, self.dev_p)

        def finish(self):
            arrive(self.low(self.opp), self.base + 2)
            arrive(self.high(self.opp), self.base + 3)

    to_y = (y, yn, yp, yo, sec(z, yn), sec(z, yp))
    to_z = (z, zn, zp, zo, sec(zn, y), sec(zp, y))

    qy_first = Cross(lambda yy, r, n: qg.at[z, yy, :, pl.ds(r, n)], *to_y, 0, 512, q_out)
    qz_first = Cross(lambda zz, r, n: qg.at[zz, y, :, pl.ds(r, n)], *to_z, 512, 512, q_out)
    qz_then = Cross(lambda zz, r, n: qg.at[zz, :, :, pl.ds(r, n)], *to_z, 0, 512, q_out_then)
    qy_then = Cross(lambda yy, r, n: qg.at[:, yy, :, pl.ds(r, n)], *to_y, 512, 512, q_out_then)
    load4.wait()
    qy_first.open()
    qz_first.open()

    load5.wait()
    for b in range(KIN // VIT):
        span = pl.ds(b * VIT, VIT)
        block = patch[:, span].astype(F32)
        centered = block - jnp.mean(block, axis=-1, keepdims=True)
        variance = jnp.mean(centered * centered, axis=-1, keepdims=True)
        rows[pl.ds(pl.multiple_of(t * ROWS, ROWS), ROWS), span] = (
            centered * lax.rsqrt(variance + 1e-06)
        ).astype(BF16)

    lane = lax.broadcasted_iota(jnp.int32, (HD, HD), 1)
    sub = lax.broadcasted_iota(jnp.int32, (HD, HD), 0)
    eye = lane == sub

    def column(row):
        return jnp.sum(jnp.where(eye, row.astype(F32), 0.0), axis=1, keepdims=True)

    def heads_down(block):
        return jnp.concatenate([block[:, h * HD : (h + 1) * HD] for h in range(8)], axis=0)

    def windows():
        counts = lens[...]
        code = jnp.zeros((1, HD), jnp.int32)
        for j in range(CITE):
            cited = cites[j : j + 1, :]
            hit = (counts > j) & ((cited // 2) == s)
            code += jnp.where(hit, 1 + (cited % 2) + 2 * (counts - 1 - j), 0)
        code = column(code)
        owned = column(prefills[...]) == (lane % NS).astype(F32)
        decode = column(decodes[...])
        codeb[NS] = jnp.sum(
            jnp.where(owned & (decode == s.astype(F32)), 1.0, 0.0), axis=0, keepdims=True
        )

        @pl.loop(0, NS)
        def _(i):
            d = ((z + i // 4) % 4) * 4 + (y + i % 4) % 4
            row = jnp.sum(jnp.where(owned & (decode == d.astype(F32)), code, 0.0), axis=0, keepdims=True)
            codeb[i] = row

    def prepare():
        @pl.loop(0, NS)
        def _(i):
            col = column(codeb[i])
            cosine, sine = qtab[0, 0:1, :], qtab[1, 0:1, :]
            for p in range(1, CITE):
                now = (col == 1.0 + 2.0 * p) | (col == 2.0 + 2.0 * p)
                cosine = jnp.where(now, qtab[0, p : p + 1, :], cosine)
                sine = jnp.where(now, qtab[1, p : p + 1, :], sine)
            asks = heads_down(qg[(z + i // 4) % 4, (y + i % 4) % 4].astype(F32))
            askb[i] = (asks * cosine + pltpu.roll(asks, HD // 2, 1) * sine).astype(BF16)

    windows()

    def w_step(b, first=False):
        part = jnp.dot(
            w2v[:, pl.ds(pl.multiple_of(b * KVB, KVB), KVB)],
            kvg[pl.ds(pl.multiple_of(b * KVB, KVB), KVB), :],
            preferred_element_type=F32,
        )
        if first:
            wacc[...] = part
        else:
            wacc[...] += part

    load2.wait()
    w_step(t, first=True)
    kv_ring.mates(0)
    w_step(mate)
    kv_ring.forward()
    row_ring = Ring(rows_at, row_out)
    row_ring.open(lambda h: rows_at(t, h))
    qy_first.forward()
    qz_first.forward()
    kv_ring.near()
    w_step(xl)
    w_step(xr)
    kv_ring.mates(1)
    w_step(2 * cl + (1 - c))
    kv_ring.mates(2)
    w_step(2 * cr + (1 - c))
    qy_first.finish()
    qz_first.finish()
    qz_then.open()
    qy_then.open()
    kv_ring.far()
    w_step(xo)
    kv_ring.mates(3)
    w_step(2 * co + (1 - c))

    def lanes(yy):
        return pl.ds(pl.multiple_of((yy % 2) * HD, HD), HD)

    def block_at(zz, yy, r0, n):
        return wg.at[zz, yy // 2, pl.ds(r0, n), lanes(yy)]

    wg[z, y // 2, :, lanes(y)] = wacc[...].astype(BF16)

    class Spread:
        def __init__(self, at, first, second, kind):
            self.at, self.kind = at, kind
            self.p, self.pn, self.pp, self.po, self.dev1n, self.dev1p = first
            self.q, self.qn, self.qp, self.qo, self.dev2n, self.dev2p = second
            self.along = (self.p, self.pp, self.pn, self.po)
            self.base = recvs.take(20)

        def whole(self, p, q):
            return self.at(p, q, 0, HALF)

        def low(self, p, q):
            return self.at(p, q, 0, QUARTER)

        def high(self, p, q):
            return self.at(p, q, QUARTER, QUARTER)

        def go(self, ref, slot, dev):
            start(ref, ref, self.kind, self.base + slot, dev)

        def across(self, k):
            block = self.whole(self.along[k], self.q)
            self.go(block, 4 + 4 * k, self.dev2n)
            self.go(block, 5 + 4 * k, self.dev2p)

        def open(self):
            block = self.whole(self.p, self.q)
            self.go(block, 0, self.dev1n)
            self.go(block, 1, self.dev1p)

        def near(self):
            arrive(self.whole(self.pp, self.q), self.base)
            self.go(self.low(self.pp, self.q), 2, self.dev1n)
            arrive(self.whole(self.pn, self.q), self.base + 1)
            self.go(self.high(self.pn, self.q), 3, self.dev1p)

        def far(self):
            arrive(self.low(self.po, self.q), self.base + 2)
            arrive(self.high(self.po, self.q), self.base + 3)
            self.across(3)

        def turn(self, k):
            p = self.along[k]
            arrive(self.whole(p, self.qp), self.base + 4 + 4 * k)
            self.go(self.low(p, self.qp), 6 + 4 * k, self.dev2n)
            arrive(self.whole(p, self.qn), self.base + 5 + 4 * k)
            self.go(self.high(p, self.qn), 7 + 4 * k, self.dev2p)

        def finish(self):
            for k in range(4):
                p = self.along[k]
                arrive(self.low(p, self.qo), self.base + 6 + 4 * k)
                arrive(self.high(p, self.qo), self.base + 7 + 4 * k)

    upper = Spread(lambda yy, zz, r, n: block_at(zz, yy, r, n), to_y, to_z, a_out)
    lower = Spread(lambda zz, yy, r, n: block_at(zz, yy, HALF + r, n), to_z, to_y, b_out)
    upper.open()
    lower.open()
    upper.across(0)
    lower.across(0)

    far_base = recvs.take(KIN // CHUNK)

    def far_part(b, k):
        return rows_at(b).at[:, pl.ds(k * CHUNK, CHUNK)]

    def far_rows():
        arrive(rows_at(xo, 0), row_ring.base + 4)
        arrive(rows_at(xo, 1), row_ring.base + 5)
        for k in range(KIN // CHUNK):
            start(far_part(xo, k), far_part(xo, k), row_out, far_base + k, to_tp(mate))

    def far_ready(k):
        arrive(far_part(2 * co + (1 - c), k), far_base + k)

    def hidden(*groups, ready=None):
        spans = [pl.ds(pl.multiple_of(g * GROUP, GROUP), GROUP) for g in groups]
        used = pl.ds(0, len(groups) * GROUP)

        def part(k):
            span = pl.ds(pl.multiple_of(k * CHUNK, CHUNK), CHUNK)
            left = jnp.concatenate([rows[r, span] for r in spans], axis=0)
            return jnp.dot(left, w1v[span, :], preferred_element_type=F32)

        if ready is None:
            hacc[used] = part(0)

            @pl.loop(1, KIN // CHUNK)
            def _(k):
                hacc[used] += part(k)
        else:
            for k in range(KIN // CHUNK):
                ready(k)
                if k == 0:
                    hacc[used] = part(k)
                else:
                    hacc[used] += part(k)

        for n, g in enumerate(groups):
            pre = hacc[n * GROUP : (n + 1) * GROUP]
            hidb[g] = (0.5 * pre * (1.0 + lax.erf(pre * np.float32(math.sqrt(0.5))))).astype(BF16)

    p_base = recvs.take(16)
    g_base = recvs.take(11)
    order = (x, cl, cr, co)
    dests = (co, cr, cl, x)

    def pair_copy(k, n):
        g = order[k]
        return remote(psend.at[g, n], precv.at[g, n], p_out, p_base + 4 * k + n, to_tp(mate))

    lower_rows, upper_rows = pl.ds(0, ROWS), pl.ds(ROWS, ROWS)
    A_R, A_L, B_R, B_L, C_L, C_R, E_R, E_L, F_R, F_L, F_O = range(11)
    places = {
        A_R: (0, lower_rows), A_L: (0, upper_rows), B_R: (1,), B_L: (2,), C_L: (pl.ds(3, 2),), C_R: (pl.ds(5, 2),),
        E_R: (7,), E_L: (8,), F_R: (9,), F_L: (10,), F_O: (11,),
    }

    def relay(m):
        who = {A_R: xr, B_R: xr, C_R: xr, E_R: xr, F_R: xr, F_O: xo}.get(m, xl)
        return remote(gsend.at[places[m]], grecv.at[places[m]], g_out, g_base + m, to_tp(who))

    def project(k):
        hid = hidb[order[k]]
        for n in range(4):
            psend[order[k], n] = jnp.dot(hid, wg[dests[n], 1 - c], preferred_element_type=F32).astype(BF16)
            pair_copy(k, n).start()
        for n in range(4):
            mine[order[k], n] = jnp.dot(hid, wg[dests[n], c], preferred_element_type=F32)

    def pair_sum(k):
        g = order[k]
        out_now = (
            {0: None},
            {0: 3, 2: 4},
            {0: 5, 1: 6},
            {0: 11, 1: 9, 2: 10},
        )[k]
        after = ({0: (A_R, A_L)}, {2: (C_L,)}, {1: (C_R,)}, {0: (F_O,), 1: (F_R,), 2: (F_L,)})[k]
        for n in range(4):
            pair_copy(k, n).wait_recv()
            total = mine[g, n] + precv[g, n].astype(F32)
            if n not in out_now:
                mine[g, n] = total
            else:
                gsend[out_now[n] or 0] = total.astype(BF16)
            for m in after.get(n, ()):
                relay(m).start()

    def pass_halves():
        relay(A_R).wait_recv()
        gsend[7, :ROWS] = (mine[cl, 1, :ROWS] + grecv[0, :ROWS].astype(F32)).astype(BF16)
        gsend[7, ROWS:] = mine[cl, 1, ROWS:].astype(BF16)
        relay(E_R).start()
        relay(A_L).wait_recv()
        gsend[8, :ROWS] = mine[cr, 2, :ROWS].astype(BF16)
        gsend[8, ROWS:] = (mine[cr, 2, ROWS:] + grecv[0, ROWS:].astype(F32)).astype(BF16)
        relay(E_L).start()

    def pass_on():
        relay(C_R).wait_recv()
        gsend[1] = (mine[x, 1] + grecv[5].astype(F32)).astype(BF16)
        relay(B_R).start()
        relay(C_L).wait_recv()
        gsend[2] = (mine[x, 2] + grecv[3].astype(F32)).astype(BF16)
        relay(B_L).start()

    def last(k):
        g = order[k]
        total = mine[g, 3]
        for m, n in (((F_O, 11), (None, 4), (None, 6)), ((B_R, 1), (F_L, 10)), ((B_L, 2), (F_R, 9)), ((E_R, 7), (E_L, 8)))[k]:
            if m is not None:
                relay(m).wait_recv()
            total += grecv[n].astype(F32)
        key = total[:, :HD]
        r = pl.ds(pl.multiple_of(g * GROUP, GROUP), GROUP)
        place = pl.ds(pl.multiple_of((g % 2) * GROUP, GROUP), GROUP)
        kbuf[r, :] = (key * ktab[0, place, :] + pltpu.roll(key, HD // 2, 1) * ktab[1, place, :]).astype(BF16)
        vt[:, r] = total[:, HD:].T.astype(BF16)

    load1.wait()
    row_ring.mates(0)
    hidden(x)
    upper.near()
    lower.near()
    for k in (1, 2):
        upper.across(k)
        lower.across(k)
    upper.turn(0)
    lower.turn(0)
    upper.far()
    lower.far()
    row_ring.forward()
    upper.turn(1)
    lower.turn(1)
    upper.turn(2)
    lower.turn(2)
    qz_then.forward()
    qy_then.forward()
    row_ring.near()
    upper.turn(3)
    lower.turn(3)
    row_ring.mates(1)
    row_ring.mates(2)
    hidden(cl, cr)
    qz_then.finish()
    qy_then.finish()
    upper.finish()
    lower.finish()
    project(0)
    project(1)
    pair_sum(0)
    project(2)
    pair_sum(1)
    far_rows()
    pair_sum(2)
    pass_halves()
    hidden(co, ready=far_ready)
    project(3)
    pass_on()
    pair_sum(3)
    prepare()
    load6.wait()
    for k in (1, 2, 3, 0):
        last(k)

    inv_root = np.float32(1.0 / math.sqrt(HD))
    o_base = recvs.take(2)

    def place(i):
        return ((z + i // 4) % 4) * 4 + (y + i % 4) % 4

    def scores_of(sections):
        asks = jnp.concatenate([askb[i] for i in sections], axis=0)
        return lax.dot_general(kbuf[...], asks, (((1,), (1,)), ((), ())), preferred_element_type=F32)

    def part_of(sections, scores):
        row = jnp.concatenate([codeb[i] for i in sections], axis=1)
        second = (row == 2.0) | (row == 4.0) | (row == 6.0) | (row == 8.0)
        frame = jnp.where(second, scores[256:], scores[:256]) * inv_root
        top = jnp.max(frame, axis=0, keepdims=True)
        weight = jnp.exp(frame - top)
        total = jnp.sum(weight, axis=0, keepdims=True)
        both = jnp.concatenate([jnp.where(second, 0.0, weight), jnp.where(second, weight, 0.0)], axis=0)
        value = jnp.dot(vt[...], both.astype(BF16), preferred_element_type=F32) / total
        live = row > 0.0
        value = jnp.where(live, value, 0.0).astype(BF16)
        level = jnp.where(live, top + jnp.log(total), -1e30)
        for k, i in enumerate(sections):
            osend[place(i)] = value[:, k * HD : (k + 1) * HD]
            lsend[place(i)] = level[:, k * HD : (k + 1) * HD]

    def part_copies(i):
        d = place(i)
        who = to_section(d)
        return (
            remote(lsend.at[d], lrecv.at[s], l_out, o_base + 1, who),
            remote(osend.at[d], orecv.at[s], o_out, o_base, who),
        )

    turns = ((10, 9, 11, 6), (14, 5, 15, 7), (13, 8, 2, 4), (12, 1, 3, 0))
    scores = scores_of(turns[0])
    for n, sections in enumerate(turns):
        now = scores
        if n + 1 < len(turns):
            scores = scores_of(turns[n + 1])
        part_of(sections, now)
        for i in sections:
            if i > 0:
                for copy in part_copies(i):
                    copy.start()
    orecv[s] = osend[s]
    lrecv[s] = lsend[s]

    asks = heads_down(q[...].astype(F32)).astype(BF16)
    own = lax.dot_general(nkv[:, :HD], asks, (((1,), (1,)), ((), ())), preferred_element_type=F32)
    pick = (lax.broadcasted_iota(jnp.int32, (NS, HD), 1) % NS) == lax.broadcasted_iota(jnp.int32, (NS, HD), 0)
    own = jnp.sum(jnp.where(pick, own, 0.0), axis=0, keepdims=True) * inv_root
    value = nkv[:, HD:].astype(F32)
    value = jnp.concatenate([value] * 8, axis=0).T
    present = codeb[NS]

    arrive(lrecv.at[pl.ds(0, NS - 1)], o_base + 1)
    arrive(orecv.at[pl.ds(0, NS - 1)], o_base)

    level = [lrecv[j] for j in range(NS)]
    top = own
    for v in level:
        top = jnp.maximum(top, v)
    weight = jnp.exp(own - top)
    total, value = weight, value * weight
    for j in range(NS):
        weight = jnp.exp(level[j] - top)
        total += weight
        value += orecv[j].astype(F32) * weight
    value = jnp.where(present > 0.0, value / total, 0.0).T
    for h in range(8):
        out[:, h * HD : (h + 1) * HD] = value[h * NS : (h + 1) * NS, :].astype(BF16)

    units = 15 * HALF
    sent(kv_out, kvg.at[pl.ds(0, 7 * KVB), :])
    sent(row_out, rows.at[pl.ds(0, 7 * ROWS), :])
    sent(q_out, qg.at[0, pl.ds(0, 3)])
    sent(q_out_then, qg.at[pl.ds(0, 3)])
    sent(a_out, kvg.at[pl.ds(0, units), :])
    sent(b_out, kvg.at[pl.ds(0, units), :])
    sent(p_out, psend)
    sent(g_out, gsend)
    sent(o_out, osend.at[pl.ds(0, NS - 1)])
    sent(l_out, lsend.at[pl.ds(0, NS - 1)])

    assert recvs.n == N_RECV, recvs.n


def shards(
    patch_states, merge_in, merge_out, kv_weight, queries, new_kv, citations, lengths, prefill_owner, decode_owner
):
    along = (1, citations.shape[0])
    keys, asks = tables()
    vmem = pl.BlockSpec(memory_space=pltpu.VMEM)
    anywhere = pl.BlockSpec(memory_space=pl.ANY)
    result = pl.pallas_call(
        kernel,
        out_shape=jax.ShapeDtypeStruct((NS, 8 * HD), BF16),
        in_specs=[anywhere] * 4 + [vmem] * 6 + [anywhere, vmem],
        out_specs=vmem,
        scratch_shapes=[
            pltpu.VMEM((ROWS, KIN), BF16),
            pltpu.VMEM((2, GRID * GRID, HD), F32),
            pltpu.VMEM((TOKENS, KIN), BF16),
            pltpu.VMEM((KIN, HU), BF16),
            pltpu.VMEM((HU, 8192), BF16),
            pltpu.VMEM((8192, HD), BF16),
            pltpu.VMEM((HU, HD), F32),
            pltpu.VMEM((4, 2, HU, 2 * HD), BF16),
            pltpu.VMEM((2 * GROUP, HU), F32),
            pltpu.VMEM((4, GROUP, HU), BF16),
            pltpu.VMEM((4, 4, GROUP, 2 * HD), F32),
            pltpu.VMEM((4, 4, GROUP, 2 * HD), BF16),
            pltpu.VMEM((4, 4, GROUP, 2 * HD), BF16),
            pltpu.VMEM((12, GROUP, 2 * HD), BF16),
            pltpu.VMEM((12, GROUP, 2 * HD), BF16),
            pltpu.VMEM((TOKENS, HD), BF16),
            pltpu.VMEM((HD, TOKENS), BF16),
            pltpu.VMEM((4, 4, NS, 8 * HD), BF16),
            pltpu.VMEM((NS, HD, HD), BF16),
            pltpu.VMEM((NS + 1, 1, HD), F32),
            pltpu.VMEM((NS, HD, HD), BF16),
            pltpu.VMEM((NS, HD, HD), BF16),
            pltpu.VMEM((NS, 1, HD), F32),
            pltpu.VMEM((NS, 1, HD), F32),
            pltpu.SemaphoreType.DMA((N_SEND,)),
            pltpu.SemaphoreType.DMA((N_RECV,)),
            pltpu.SemaphoreType.DMA((N_LOCAL,)),
        ],
        compiler_params=pltpu.CompilerParams(
            collective_id=0, has_side_effects=True, vmem_limit_bytes=58 * 1024 * 1024
        ),
    )(
        patch_states, merge_in, merge_out, kv_weight, queries[0], new_kv[0],
        citations.T, lengths.reshape(along), prefill_owner.reshape(along), decode_owner.reshape(along),
        jnp.asarray(keys), jnp.asarray(asks),
    )
    return result[None]


def solution(mesh):
    return jax.shard_map(
        shards,
        mesh=mesh,
        in_specs=(
            P(("section", "tp"), None),
            P(None, "tp"),
            P("tp", None),
            P("tp", None),
            P("section", None, "tp"),
            P("section", None, "tp"),
            P(),
            P(),
            P(),
            P(),
        ),
        out_specs=P("section", None, "tp"),
        check_vma=False,
    )
```

time: 83.9 us -> 67 us (0.80)
  Pallas kernels: 80.9 us -> 65.2 us
  local copies, waits for them, and re-layouts: 2.84 us -> 1.38 us
    pallas_call x1, Pallas kernels: 80.9 us -> 65.2 us  [shards(): pl.pallas_call(kernel, out_shape=jax.ShapeDtypeStruct((NS, 8 * HD), BF16)...]
    concatenate x2 -> x0, local copies, waits for them, and re-layouts: 1.47 us -> none  [shards(): jnp.concatenate([citations, lengths[:, None], prefill_owner[:, None], dec...]
where the time goes in v3:
time: 67 us; the launch traced here: 66.5 us
  Pallas kernels  65.2 us (97%)
  local copies, waits for them, and re-layouts  1.38 us (2%)
    pallas_call x1, Pallas kernels, shards(): pl.pallas_call(kernel, out_shape=jax.ShapeDtypeStruct((NS, 8 * HD), BF16)...  65.2 us
    unnamed x1, local copies, waits for them, and re-layouts  1.38 us

profile of v3, /device:TPU:1, one launch (start us, length us, event | category | flops | bytes accessed | tf_op | source)
XLA Modules:
  0.0 66.5 jit_solution(4552413920964921451)
XLA Ops:
  0.0 65.2 %shard_map.118 = bf16[16,1024]{1,0:T(8,128)(2,1)} custom-call(bf16[64,5120]{1,0:T(8,128)(2,1)} %patch_in.1, bf16[5120,640]{1,0:T(8,128)(2,1)} %w1.1, bf16[640,8192]{1,0:T(8,128)(2,1)} %w2.1, bf16[1024,2048]{1,0:T(8,128)(2,1)} %kvw.1, bf16[16,1024]{1,0:T(8,128)(2,1)} %bitcast.8, bf16[16,256]{1,0:T(8,128)(2,1)} %bitcast.9, s32[4,128]{1,0:T(4,128)} %bitcast.10, ...), custom_call_target="tpu_custom_call" | custom-call | tf_op jit(solution)/shard_map/pallas_call | solution.py:638
  65.2 1.4 %copy.14 = bf16[1,16,1024]{2,1,0:T(8,128)(2,1)} copy(bf16[1,16,1024]{2,1,0:T(8,128)(2,1)} %bitcast.7) | data formatting | bytes 65536

commit v4 on v3

--- a/solution.py
+++ b/solution.py
@@ -528,8 +528,8 @@
     pair_sum(0)
     project(2)
     pair_sum(1)
+    pair_sum(2)
     far_rows()
-    pair_sum(2)
     pass_halves()
     hidden(co, ready=far_ready)
     project(3)

time: 67 us -> 68.2 us (1.018)
  Pallas kernels: 65.2 us -> 66.6 us
    pallas_call x1, Pallas kernels: 65.2 us -> 66.6 us  [shards(): pl.pallas_call(kernel, out_shape=jax.ShapeDtypeStruct((NS, 8 * HD), BF16)...]
where the time goes in v4:
time: 68.2 us; the launch traced here: 68 us
  Pallas kernels  66.6 us (98%)
  local copies, waits for them, and re-layouts  1.38 us (2%)
    pallas_call x1, Pallas kernels, shards(): pl.pallas_call(kernel, out_shape=jax.ShapeDtypeStruct((NS, 8 * HD), BF16)...  66.6 us
    unnamed x1, local copies, waits for them, and re-layouts  1.38 us

profile of v4, /device:TPU:1, one launch (start us, length us, event | category | flops | bytes accessed | tf_op | source)
XLA Modules:
  0.0 68.0 jit_solution(4836520630708248043)
XLA Ops:
  0.0 66.6 %shard_map.118 = bf16[16,1024]{1,0:T(8,128)(2,1)} custom-call(bf16[64,5120]{1,0:T(8,128)(2,1)} %patch_in.1, bf16[5120,640]{1,0:T(8,128)(2,1)} %w1.1, bf16[640,8192]{1,0:T(8,128)(2,1)} %w2.1, bf16[1024,2048]{1,0:T(8,128)(2,1)} %kvw.1, bf16[16,1024]{1,0:T(8,128)(2,1)} %bitcast.8, bf16[16,256]{1,0:T(8,128)(2,1)} %bitcast.9, s32[4,128]{1,0:T(4,128)} %bitcast.10, ...), custom_call_target="tpu_custom_call" | custom-call | tf_op jit(solution)/shard_map/pallas_call | solution.py:638
  66.6 1.4 %copy.14 = bf16[1,16,1024]{2,1,0:T(8,128)(2,1)} copy(bf16[1,16,1024]{2,1,0:T(8,128)(2,1)} %bitcast.7) | data formatting | bytes 65536
